TPU v7x, 32 devices: a whole 2x2x4 slice. The times are simulated.
32 devices in a mesh: groups: 1, ctx: 8 (over z, y), bal: 4 (over x, core), head: 1.
Axes of the slice: x: 2, y: 2, z: 4, core: 2. Of those that a mesh axis runs over, the one named last changes fastest.
Arguments:
- queries: bfloat16 [16384, 2560], P(('groups', 'ctx', 'bal'), 'head'), may hold values from -32 to 32
- keys: bfloat16 [16384, 2560], P(('groups', 'ctx', 'bal'), 'head'), may hold values from -32 to 32
- values: bfloat16 [16384, 2560], P(('groups', 'ctx', 'bal'), 'head'), may hold values from -6 to 6
- output_gradient: bfloat16 [16384, 2560], P(('groups', 'ctx', 'bal'), 'head'), may hold values from -6 to 6
- dilation_phase: int32 [20], P('head'), may hold values from 0 to 127
- segment_device_count: int32 [20], P('head'), may hold values from 1 to 32, as said below
- owner: int32 [128], P('groups'), may hold values from 0 to 127, as said below
Outputs:
- attended: bfloat16 [16384, 2560], P(('groups', 'ctx', 'bal'), 'head')
- query_grad: bfloat16 [16384, 2560], P(('groups', 'ctx', 'bal'), 'head')
- key_grad: bfloat16 [16384, 2560], P(('groups', 'ctx', 'bal'), 'head')
- value_grad: bfloat16 [16384, 2560], P(('groups', 'ctx', 'bal'), 'head')
Inputs may be any that keep to these rules, and one draw needn't show every extreme that they name: `segment_device_count`: every entry is a power of two. The device at index d of the 32 devices of a document (context shard major) holds blocks d * 4 onward. owner is one to one and keeps every block in its context shard of 4 devices: a block of the device at index b of a shard goes to some device e of that shard, into its slot b + t with 0 <= t < 1, and every device hands exactly 1 of its blocks to each device of its shard, itself included.
All inputs are finite; a program needn't handle non-finite values.
Results may differ from a plain program's by a relative error of at most 0.013.
The roundings to bfloat16 on the way count: a program that leaves them out, or rounds other values in their place, can miss the bound.
Values may be sent and summed in bfloat16 or wider, within the bound.
No kernel may reach another device: no remote copies, remote signals or barrier semaphores. Data moves between devices by JAX's collectives and lax.ppermute only.
A program may use at most 128 MiB of HBM per device.

v0:
```python
import functools
import math

import jax
import jax.numpy as jnp
from jax import lax
from jax.experimental import pallas as pl
from jax.experimental.pallas import tpu as pltpu
from jax.sharding import PartitionSpec as P

BLOCK = 128
HEAD = 128
LOG2E = 1.4426950408889634
NT = (((1,), (1,)), ((), ()))
TN = (((0,), (0,)), ((), ()))


def tables(positions, total):
    half = HEAD // 2
    pair = jnp.arange(half, dtype=jnp.float32)
    inverse = jnp.exp(pair * (-2.0 * math.log(10000.0) / HEAD))
    where = positions.astype(jnp.float32)[..., None]
    angles = where * inverse
    base = (2.0 * pair / HEAD + 0.4) / 1.4
    growth = jnp.exp((2.0 * where - total) / total * jnp.log(base))
    cosine, sine = jnp.cos(angles), jnp.sin(angles)

    def pack(scale):
        first, second = cosine * scale, sine * scale
        return (
            jnp.concatenate([first, first], axis=-1),
            jnp.concatenate([-second, second], axis=-1),
        )

    return pack(growth) + pack(1.0 / growth)


def dot(left, right, dims=None):
    if dims is None:
        dims = (((1,), (0,)), ((), ()))
    return lax.dot_general(left, right, dims, preferred_element_type=jnp.float32)


def attend_kernel(
    per_step, blocks, count, first, relaid, info, phase, seg, far_ref, pull_ref, push_ref, *rest
):
    cq_ref, sq_ref, ck_ref, sk_ref = rest[:4]
    own = rest[4:8]
    rest = rest[8:]
    if relaid:
        come, rest = rest[: blocks - 1], rest[blocks:]
        finals, rest = rest[:4], rest[4:]
    else:
        finals, rest = rest[:blocks], rest[blocks:]
    pay_ref, near_k, near_v, far_sum = rest
    scale = 1.0 / math.sqrt(HEAD)
    key_at = lax.broadcasted_iota(jnp.int32, (BLOCK, BLOCK), 0)
    query_at = lax.broadcasted_iota(jnp.int32, (BLOCK, BLOCK), 1)
    causal = key_at <= query_at
    far_at = lax.broadcasted_iota(jnp.int32, (count, BLOCK), 0)
    half = HEAD // 2
    for sub in range(per_step):
        head = first + pl.program_id(0) * per_step + sub
        lanes = slice(sub * HEAD, (sub + 1) * HEAD)
        both = dot(pull_ref[...], far_ref[:, lanes]).astype(jnp.bfloat16)
        far_k, far_v = both[:count], both[count:]
        span = seg[head] * blocks
        p_far, d_far, q_all, g_all = [], [], [], []
        for k in range(blocks):
            if relaid:
                rows = slice(k * BLOCK, (k + 1) * BLOCK)
                source = [ref[:, lanes] for ref in own]
                if k:
                    source = [come[k - 1][t, :, lanes] for t in range(4)]
            else:
                rows = pl.ds(pl.multiple_of(info[k] * BLOCK, BLOCK), BLOCK)
                source = [ref[rows, lanes] for ref in own]
            block = info[blocks + k]
            low = block & (-span)
            cq, sq, ck, sk = cq_ref[rows, :], sq_ref[rows, :], ck_ref[rows, :], sk_ref[rows, :]
            raw_q, raw_k, value, grad = source
            raw_q = raw_q.astype(jnp.float32)
            raw_k = raw_k.astype(jnp.float32)
            tq = (raw_q * cq + pltpu.roll(raw_q, half, 1) * sq).astype(jnp.bfloat16)
            tk = (raw_k * ck + pltpu.roll(raw_k, half, 1) * sk).astype(jnp.bfloat16)
            keys = jnp.concatenate([tk, far_k], axis=0)
            vals = jnp.concatenate([value, far_v], axis=0)
            score = dot(keys, tq, NT)
            allowed = (far_at >= low) & (far_at < block)
            score = jnp.concatenate(
                [
                    jnp.where(causal, score[:BLOCK], -jnp.inf),
                    jnp.where(allowed, score[BLOCK:], -jnp.inf),
                ],
                axis=0,
            )
            top = jnp.max(score, axis=0, keepdims=True)
            weight = jnp.exp2((score - top) * (scale * LOG2E))
            prob = weight * (1.0 / jnp.sum(weight, axis=0, keepdims=True))
            p16 = prob.astype(jnp.bfloat16)
            dprob = dot(vals, grad, NT)
            delta = jnp.sum(p16.astype(jnp.float32) * dprob, axis=0, keepdims=True)
            d16 = (prob * (dprob - delta)).astype(jnp.bfloat16)
            out = dot(p16, vals, TN)
            dq = dot(d16, keys, TN) * scale
            dk = dot(d16[:BLOCK], tq) * scale
            dv = dot(p16[:BLOCK], grad)
            near_k[k] = dk
            near_v[k] = dv
            made = (
                out,
                dq * cq - pltpu.roll(dq, half, 1) * sq,
                dk * ck - pltpu.roll(dk, half, 1) * sk,
                dv,
            )
            for t in range(4):
                if relaid:
                    finals[t][info[2 * blocks + k], :, lanes] = made[t].astype(jnp.bfloat16)
                else:
                    finals[k][t, :, lanes] = made[t].astype(jnp.bfloat16)
            p_far.append(p16[BLOCK:])
            d_far.append(d16[BLOCK:])
            q_all.append(tq)
            g_all.append(grad)
        far_sum[:count] = (
            dot(jnp.concatenate(d_far, axis=1), jnp.concatenate(q_all, axis=0)) * scale
        )
        far_sum[count:] = dot(jnp.concatenate(p_far, axis=1), jnp.concatenate(g_all, axis=0))
        at = phase[head]
        for k in range(blocks):
            block = info[blocks + k]
            far_sum[pl.ds(block, 1), :] = far_sum[pl.ds(block, 1), :] + near_k[k, pl.ds(at, 1), :]
            far_sum[pl.ds(count + block, 1), :] = (
                far_sum[pl.ds(count + block, 1), :] + near_v[k, pl.ds(at, 1), :]
            )
        pay_ref[:, lanes] = dot(push_ref[...], far_sum[...].astype(jnp.bfloat16)).astype(
            jnp.bfloat16
        )


def pick_kernel(heads, blocks, phase, k_hbm, v_hbm, cos_ref, sin_ref, out_ref, k_ref, v_ref, load):
    moves = [
        pltpu.make_async_copy(k_hbm, k_ref, load.at[0]),
        pltpu.make_async_copy(v_hbm, v_ref, load.at[1]),
    ]
    for move in moves:
        move.start()
    spot = lax.broadcasted_iota(jnp.int32, (16, HEAD), 0)
    for t in range(2):
        moves[t].wait()
        ref = (k_ref, v_ref)[t]
        for head in range(heads):
            at = phase[head]
            start = pl.multiple_of(at // 16 * 16, 16)
            lanes = slice(head * HEAD, (head + 1) * HEAD)
            rows = []
            for k in range(blocks):
                tile = ref[pl.ds(pl.multiple_of(k * BLOCK + start, 16), 16), lanes]
                tile = jnp.where(spot == at - start, tile.astype(jnp.float32), 0.0)
                rows.append(jnp.sum(tile, axis=0, keepdims=True))
            row = jnp.concatenate(rows, axis=0)
            if t == 0:
                row = row * cos_ref[:, lanes] + pltpu.roll(row, HEAD // 2, 1) * sin_ref[:, lanes]
            out_ref[t * blocks : (t + 1) * blocks, lanes] = row


def pack_kernel(blocks, width, info, far_ref, *rest):
    inputs = rest[:4]
    outs = rest[4 : 4 + blocks - 1]
    sems = rest[4 + blocks - 1]
    for wait in (False, True):
        for k in reversed(range(1, blocks)):
            rows = pl.ds(pl.multiple_of(info[k] * BLOCK, BLOCK), BLOCK)
            for t in range(4):
                move = pltpu.make_async_copy(
                    inputs[t].at[rows, pl.ds(0, width)], outs[k - 1].at[t], sems.at[k - 1, t]
                )
                if wait:
                    move.wait()
                else:
                    move.start()


def finish_kernel(heads, blocks, first, phase, slot, got_ref, cos_ref, sin_ref, *rest):
    parts = rest[:blocks]
    finals = rest[blocks + 4 : blocks + 8]
    room, left, load, save, take, give = rest[blocks + 8 :]
    edge = first * HEAD

    def rows(k):
        return pl.ds(k * BLOCK, BLOCK)

    loads = [pltpu.make_async_copy(parts[k], room.at[slot[k]], load.at[k]) for k in range(blocks)]
    takes = [
        pltpu.make_async_copy(finals[2 + t].at[:, pl.ds(0, edge)], left.at[t], take.at[t])
        for t in range(2)
    ]
    gives = [
        pltpu.make_async_copy(left.at[t], finals[2 + t].at[:, pl.ds(0, edge)], give.at[t])
        for t in range(2)
    ]
    saves = [
        [
            pltpu.make_async_copy(
                room.at[k, t], finals[t].at[rows(k), pl.ds(edge, room.shape[-1])], save.at[t, k]
            )
            for k in range(blocks)
        ]
        for t in range(4)
    ]
    for move in loads + takes:
        move.start()
    senders = got_ref.shape[0]
    total = got_ref[0].astype(jnp.float32)
    for sender in range(1, senders):
        total = total + got_ref[sender].astype(jnp.float32)
    far_k, far_v = total[:blocks], total[blocks:]
    for move in loads:
        move.wait()
    for t in range(2):
        for move in saves[t]:
            move.start()
    for move in takes:
        move.wait()
    spot = lax.broadcasted_iota(jnp.int32, (16, HEAD), 0)
    for head in range(heads):
        at = phase[head]
        start = pl.multiple_of(at // 16 * 16, 16)
        lanes = slice(head * HEAD, (head + 1) * HEAD)
        turned = far_k[:, lanes] * cos_ref[:, lanes] - pltpu.roll(
            far_k[:, lanes], HEAD // 2, 1
        ) * sin_ref[:, lanes]
        for k in range(blocks):
            for t, row in ((0, turned[k : k + 1]), (1, far_v[k : k + 1, lanes])):
                if head < first:
                    spots = pl.ds(pl.multiple_of(k * BLOCK + start, 16), 16)
                    old = left[t, spots, lanes]
                else:
                    here = slice((head - first) * HEAD, (head - first + 1) * HEAD)
                    old = room[k, t + 2, pl.ds(start, 16), here]
                new = jnp.where(spot == at - start, row, old.astype(jnp.float32)).astype(
                    jnp.bfloat16
                )
                if head < first:
                    left[t, spots, lanes] = new
                else:
                    room[k, t + 2, pl.ds(start, 16), here] = new
    for t in range(2, 4):
        for move in saves[t]:
            move.start()
    for move in gives:
        move.start()
    for t in range(4):
        for move in saves[t]:
            move.wait()
    for move in gives:
        move.wait()


def local(queries, keys, values, output_gradient, dilation_phase, segment_device_count, owner):
    rows, width = queries.shape
    heads = width // HEAD
    blocks = rows // BLOCK
    bal_size = lax.axis_size("bal")
    devices = lax.axis_size("ctx") * bal_size
    total = rows * devices
    count = owner.shape[0]
    assert blocks == bal_size and bal_size & (bal_size - 1) == 0
    bal = lax.axis_index("bal")
    device = lax.axis_index("ctx") * bal_size + bal
    big = pltpu.CompilerParams(vmem_limit_bytes=50 * 1024 * 1024)
    smem = pl.BlockSpec(memory_space=pltpu.SMEM)
    vmem = pl.BlockSpec(memory_space=pltpu.VMEM)
    anywhere = pl.BlockSpec(memory_space=pl.ANY)

    def tokens_of(ids):
        return (ids[:, None] * BLOCK + jnp.arange(BLOCK, dtype=jnp.int32)[None, :]).reshape(rows)

    def swap(array, k):
        return lax.ppermute(array, "bal", [(i, i ^ k) for i in range(bal_size)])

    steps = jnp.arange(blocks, dtype=jnp.int32)
    held = device * blocks + steps
    goes_to = lax.dynamic_slice_in_dim(owner, device * blocks, blocks) // blocks % bal_size
    partner = steps ^ bal
    which = jnp.sum(jnp.where(goes_to[None, :] == partner[:, None], steps[None, :], 0), axis=1)
    info = jnp.concatenate([which, device * blocks + which]).astype(jnp.int32)
    comes_from = jnp.sum(
        jnp.where(
            owner[None, :] == held[:, None], jnp.arange(count, dtype=jnp.int32)[None, :], 0
        ),
        axis=1,
    )

    cq, sq, ck, sk = tables(tokens_of(held), total)
    own_phase = (held[:, None] * BLOCK + dilation_phase[None, :]).astype(jnp.int32)
    _, _, pick_cos, pick_sin = tables(own_phase, total)
    own_far = pl.pallas_call(
        functools.partial(pick_kernel, heads, blocks),
        in_specs=[smem, anywhere, anywhere, vmem, vmem],
        out_specs=vmem,
        out_shape=jax.ShapeDtypeStruct((2 * blocks, width), jnp.float32),
        scratch_shapes=[
            pltpu.VMEM((rows, width), jnp.bfloat16),
            pltpu.VMEM((rows, width), jnp.bfloat16),
            pltpu.SemaphoreType.DMA((2,)),
        ],
        compiler_params=big,
    )(
        dilation_phase,
        keys,
        values,
        pick_cos.reshape(blocks, width),
        pick_sin.reshape(blocks, width),
    ).astype(jnp.bfloat16)
    far = lax.all_to_all(
        jnp.broadcast_to(own_far[None], (devices, 2 * blocks, width)),
        ("ctx", "bal"),
        split_axis=0,
        concat_axis=0,
        tiled=True,
    ).reshape(devices * 2 * blocks, width)

    first = heads // 4 * 2
    last = heads - first
    edge = first * HEAD
    sent = pl.pallas_call(
        functools.partial(pack_kernel, blocks, edge),
        in_specs=[smem] + [anywhere] * 5,
        out_specs=[anywhere] * (blocks - 1),
        out_shape=[jax.ShapeDtypeStruct((4, BLOCK, edge), jnp.bfloat16)] * (blocks - 1),
        scratch_shapes=[pltpu.SemaphoreType.DMA((blocks - 1, 4))],
        compiler_params=big,
    )(info, own_far, queries, keys, values, output_gradient)
    come = [swap(sent[k - 1], k) for k in range(1, blocks)]

    side = 2 * count
    wide = jnp.arange(side, dtype=jnp.int32)
    tall = wide[:, None]
    wide = wide[None, :]
    source = tall % count
    pull = (
        wide == source // blocks * (2 * blocks) + tall // count * blocks + source % blocks
    ).astype(jnp.bfloat16)
    lands = owner // blocks * (2 * blocks) + owner % blocks
    push = (jnp.concatenate([lands, lands + blocks])[None, :] == tall).astype(jnp.bfloat16)

    per_step = 2
    columns = per_step * HEAD
    fixed = lambda h, *_: (0, 0)
    square = pl.BlockSpec((side, side), fixed)
    table = pl.BlockSpec((rows, HEAD), fixed)
    part = pl.BlockSpec((4, BLOCK, columns), lambda h, *_: (0, 0, h))
    scratch = [
        pltpu.VMEM((blocks, BLOCK, HEAD), jnp.float32),
        pltpu.VMEM((blocks, BLOCK, HEAD), jnp.float32),
        pltpu.VMEM((side, HEAD), jnp.float32),
    ]
    originals = (queries, keys, values, output_gradient)

    skip = first // per_step
    tensor = pl.BlockSpec((rows, columns), lambda h, *_: (0, h + skip))
    lane = pl.BlockSpec((side, columns), lambda h, *_: (0, h + skip))
    results = pl.pallas_call(
        functools.partial(attend_kernel, per_step, blocks, count, first, False),
        grid_spec=pltpu.PrefetchScalarGridSpec(
            num_scalar_prefetch=3,
            grid=(last // per_step,),
            in_specs=[lane, square, square] + [table] * 4 + [tensor] * 4,
            out_specs=[part] * blocks + [lane],
            scratch_shapes=scratch,
        ),
        out_shape=[jax.ShapeDtypeStruct((4, BLOCK, last * HEAD), jnp.bfloat16)] * blocks
        + [jax.ShapeDtypeStruct((side, width), jnp.bfloat16)],
        compiler_params=big,
    )(info, dilation_phase, segment_device_count, far, pull, push, cq, sq, ck, sk, *originals)
    parts, payload = list(results[:blocks]), results[blocks]
    for k in range(1, blocks):
        parts[k] = swap(parts[k], k)

    ids = (device ^ steps) * blocks
    came = jnp.sum(
        jnp.where(comes_from[None, :] // blocks * blocks == ids[:, None], comes_from[None, :], 0),
        axis=1,
    )
    moved = jnp.concatenate([which, came, partner]).astype(jnp.int32)
    cq, sq, ck, sk = tables(tokens_of(came), total)
    tensor = pl.BlockSpec((BLOCK, columns), lambda h, info, *_: (info[0], h))
    lane = pl.BlockSpec((side, columns), lambda h, *_: (0, h))
    whole = pl.BlockSpec((blocks, BLOCK, columns), lambda h, *_: (0, 0, h))
    results = pl.pallas_call(
        functools.partial(attend_kernel, per_step, blocks, count, 0, True),
        grid_spec=pltpu.PrefetchScalarGridSpec(
            num_scalar_prefetch=3,
            grid=(first // per_step,),
            in_specs=[lane, square, square]
            + [table] * 4
            + [tensor] * 4
            + [part] * (blocks - 1)
            + [anywhere],
            out_specs=[whole] * 4 + [lane],
            scratch_shapes=scratch,
        ),
        out_shape=[jax.ShapeDtypeStruct((blocks, BLOCK, width), jnp.bfloat16)] * 4
        + [jax.ShapeDtypeStruct((side, width), jnp.bfloat16)],
        input_output_aliases={3 + 3 + 4 + 4 + blocks - 1: 4},
        compiler_params=big,
    )(
        moved,
        dilation_phase,
        segment_device_count,
        far,
        pull,
        push,
        cq,
        sq,
        ck,
        sk,
        *originals,
        *come,
        payload,
    )
    finals, payload = [one.reshape(rows, width) for one in results[:4]], results[4]
    got = lax.all_to_all(
        payload.reshape(devices, 2 * blocks, width),
        ("ctx", "bal"),
        split_axis=0,
        concat_axis=0,
        tiled=True,
    )

    new_phase = (comes_from[:, None] * BLOCK + dilation_phase[None, :]).astype(jnp.int32)
    _, _, new_cos, new_sin = tables(new_phase, total)
    return tuple(
        pl.pallas_call(
            functools.partial(finish_kernel, heads, blocks, first),
            in_specs=[smem, smem, vmem, vmem, vmem] + [anywhere] * (blocks + 4),
            out_specs=[anywhere] * 4,
            out_shape=[jax.ShapeDtypeStruct((rows, width), jnp.bfloat16)] * 4,
            input_output_aliases={5 + blocks + t: t for t in range(4)},
            scratch_shapes=[
                pltpu.VMEM((blocks, 4, BLOCK, last * HEAD), jnp.bfloat16),
                pltpu.VMEM((2, rows, edge), jnp.bfloat16),
                pltpu.SemaphoreType.DMA((blocks,)),
                pltpu.SemaphoreType.DMA((4, blocks)),
                pltpu.SemaphoreType.DMA((2,)),
                pltpu.SemaphoreType.DMA((2,)),
            ],
            compiler_params=big,
        )(
            dilation_phase,
            partner.astype(jnp.int32),
            got,
            new_cos.reshape(blocks, width),
            new_sin.reshape(blocks, width),
            *parts,
            *finals,
        )
    )


def solution(mesh):
    token = P(("groups", "ctx", "bal"), "head")
    return jax.shard_map(
        local,
        mesh=mesh,
        in_specs=(token, token, token, token, P("head"), P("head"), P("groups")),
        out_specs=(token, token, token, token),
        check_vma=False,
    )
```

profile of v0, /device:TPU:0, one launch (start us, length us, event | category | flops | bytes accessed | tf_op | source)
XLA Modules:
  0.0 310.6 jit_solution(1383089442672405148)
XLA Ops:
  3.0 1.1 fusion.20
  4.3 1.7 copy-done
  6.6 2.7 shard_map.102
  9.3 1.1 broadcast_in_dim.41
  10.5 7.3 %all-to-all-start = ((bf16[32,8,2560]{2,1,0:T(8,128)(2,1)}), bf16[32,8,2560]{2,1,0:T(8,128)(2,1)S(1)}, u32[]{:S(2)}, u32[]{:S(2)}) async-start(bf16[32,8,2560]{2,1,0:T(8,128)(2,1)} %broadcast_in_dim.41), calls=%async_computation | async-start | bytes 2621440 | tf_op jit(solution)/shard_map/all_to_all | solution.py:316
  18.2 120.9 %shard_map.103 = (bf16[4,128,1280]{2,1,0:T(8,128)(2,1)}, bf16[4,128,1280]{2,1,0:T(8,128)(2,1)}, bf16[4,128,1280]{2,1,0:T(8,128)(2,1)}) custom-call(s32[8]{0:T(128)S(1)} %pad_add_fusion.2.info, bf16[8,2560]{1,0:T(8,128)(2,1)S(1)} %convert_element_type.58.far_ref, bf16[512,2560]{1,0:T(8,128)(2,1)} %rest_4_.3, bf16[512,2560]{1,0:T(8,128)(2,1)} %rest_5_.3, ...), custom_call_target="tpu_custom_call" | custom-call | tf_op jit(solution)/shard_map/pallas_call | solution.py:327
  139.4 1.7 collective-permute-start.1
  141.6 2.1 fusion.13
  143.7 0.8 pad_maximum_fusion.4.rest_0_
  146.3 0.9 pad_maximum_fusion.2.rest_2_
  147.1 0.8 pad_maximum_fusion.7.rest_3_
  149.2 1.0 copy-done.1
  150.3 0.9 copy-done.9
  151.2 0.9 copy-done.10
  152.2 0.9 copy-done.11
  153.1 0.9 copy-done.12
  154.1 22.6 %shard_map.104 = (bf16[4,128,1280]{2,1,0:T(8,128)(2,1)S(1)}, bf16[4,128,1280]{2,1,0:T(8,128)(2,1)S(1)}, bf16[4,128,1280]{2,1,0:T(8,128)(2,1)}, bf16[4,128,1280]{2,1,0:T(8,128)(2,1)}, bf16[256,2560]{1,0:T(8,128)(2,1)}) custom-call(s32[8]{0:T(128)S(1)} %pad_add_fusion.2.info, s32[20]{0:T(128)S(1)} %copy-done.14, s32[20]{0:T(128)S(1)} %copy-done.15, ...), custom_call_target="tpu_custom_call" | custom-call | tf_op jit(solution)/shard_map/pallas_call | solution.py:364
  176.7 1.1 copy-done.16
  177.7 20.4 %collective-permute-done.2.rest_10_ = bf16[4,128,1280]{2,1,0:T(8,128)(2,1)} collective-permute-done((bf16[4,128,1280]{2,1,0:T(8,128)(2,1)}, bf16[4,128,1280]{2,1,0:T(8,128)(2,1)}, u32[]{:S(2)}, u32[]{:S(2)}) %collective-permute-start.2) | collective-permute-done | bytes 1310752 | tf_op jit(solution)/shard_map/ppermute | solution.py:280
  198.1 1.3 copy-done.2
  199.4 1.3 copy-done.3
  200.7 22.7 %shard_map.105 = (bf16[4,128,2560]{2,1,0:T(8,128)(2,1)}, bf16[4,128,2560]{2,1,0:T(8,128)(2,1)}, bf16[4,128,2560]{2,1,0:T(8,128)(2,1)}, bf16[4,128,2560]{2,1,0:T(8,128)(2,1)}, bf16[256,2560]{1,0:T(8,128)(2,1)S(1)}) custom-call(s32[12]{0:T(128)S(1)} %pad_add_fusion.1.info, s32[20]{0:T(128)S(1)} %copy-done.14, ...), custom_call_target="tpu_custom_call", output_to_operand_aliasing={{4}: (17, {})} | custom-call | tf_op jit(solution)/shard_map/pallas_call | solution.py:391
  223.4 1.1 copy-done.4
  224.5 5.9 %all-to-all-start.1 = ((bf16[32,8,2560]{2,1,0:T(8,128)(2,1)}), bf16[32,8,2560]{2,1,0:T(8,128)(2,1)S(1)}, u32[]{:S(2)}, u32[]{:S(2)}) async-start(bf16[32,8,2560]{2,1,0:T(8,128)(2,1)} %bitcast.36), calls=%async_computation.1 | async-start | bytes 2621440 | tf_op jit(solution)/shard_map/all_to_all | solution.py:424
  230.7 1.7 collective-permute-start.4
  232.6 1.1 collective-permute-done.3.rest_1_
  233.7 1.1 copy-done.5
  234.8 41.1 %collective-permute-done.4.rest_2_ = bf16[4,128,1280]{2,1,0:T(8,128)(2,1)S(1)} collective-permute-done((bf16[4,128,1280]{2,1,0:T(8,128)(2,1)}, bf16[4,128,1280]{2,1,0:T(8,128)(2,1)S(1)}, u32[]{:S(2)}, u32[]{:S(2)}) %collective-permute-start.4) | collective-permute-done | bytes 1310752 | tf_op jit(solution)/shard_map/ppermute | solution.py:280
  275.8 1.1 copy-done.17
  276.9 26.2 %collective-permute-done.5.rest_3_ = bf16[4,128,1280]{2,1,0:T(8,128)(2,1)} collective-permute-done((bf16[4,128,1280]{2,1,0:T(8,128)(2,1)}, bf16[4,128,1280]{2,1,0:T(8,128)(2,1)}, u32[]{:S(2)}, u32[]{:S(2)}) %collective-permute-start.5) | collective-permute-done | bytes 1310752 | tf_op jit(solution)/shard_map/ppermute | solution.py:280
  303.1 1.3 copy-done.6
  304.4 6.2 %shard_map.106 = (bf16[512,2560]{1,0:T(8,128)(2,1)}, bf16[512,2560]{1,0:T(8,128)(2,1)}, bf16[512,2560]{1,0:T(8,128)(2,1)}, bf16[512,2560]{1,0:T(8,128)(2,1)}) custom-call(s32[20]{0:T(128)S(1)} %copy-done.14, s32[4]{0:T(128)S(1)} %iota_xor_fusion.slot, ...), custom_call_target="tpu_custom_call", output_to_operand_aliasing={{0}: (9, {}), {1}: (10, {}), {2}: (11, {}), {3}: (12, {})} | custom-call | tf_op jit(solution)/shard_map/pallas_call | solution.py:435
  (72 shorter events, 7.9 us)
Async XLA Ops:
  4.2 1.7 copy-start
  6.0 0.7 copy-start.13
  10.5 7.3 %copy-start.19 = (s32[128]{0:T(128)S(1)}, s32[128]{0:T(128)}, u32[]{:S(2)}) copy-start(s32[128]{0:T(128)} %param.13) | copy-start | bytes 1540
  10.5 138.7 %all-to-all-start = ((bf16[32,8,2560]{2,1,0:T(8,128)(2,1)}), bf16[32,8,2560]{2,1,0:T(8,128)(2,1)S(1)}, u32[]{:S(2)}, u32[]{:S(2)}) async-start(bf16[32,8,2560]{2,1,0:T(8,128)(2,1)} %broadcast_in_dim.41), calls=%async_computation | async-start | bytes 2621440 | tf_op jit(solution)/shard_map/all_to_all | solution.py:316
  139.0 38.7 %collective-permute-start = (bf16[4,128,1280]{2,1,0:T(8,128)(2,1)}, bf16[4,128,1280]{2,1,0:T(8,128)(2,1)}, u32[]{:S(2)}, u32[]{:S(2)}) collective-permute-start(bf16[4,128,1280]{2,1,0:T(8,128)(2,1)} %get-tuple-element.17), channel_id=1, source_target_pairs={{0,1},{1,0},{2,3},{3,2},{4,5},{5,4},{6,7},{7,6},{8,9},{9,8},{10,11... | collective-permute-start | bytes 3932168 | tf_op jit(solution)/shard_map/ppermute | solution.py:280
  139.4 38.4 %collective-permute-start.1 = (bf16[4,128,1280]{2,1,0:T(8,128)(2,1)}, bf16[4,128,1280]{2,1,0:T(8,128)(2,1)}, u32[]{:S(2)}, u32[]{:S(2)}) collective-permute-start(bf16[4,128,1280]{2,1,0:T(8,128)(2,1)} %get-tuple-element.18), channel_id=1, source_target_pairs={{0,2},{1,3},{2,0},{3,1},{4,6},{5,7},{6,4},{7,5},{8,10},{9,11},{10,... | collective-permute-start | bytes 3932168 | tf_op jit(solution)/shard_map/ppermute | solution.py:280
  141.0 57.0 %collective-permute-start.2 = (bf16[4,128,1280]{2,1,0:T(8,128)(2,1)}, bf16[4,128,1280]{2,1,0:T(8,128)(2,1)}, u32[]{:S(2)}, u32[]{:S(2)}) collective-permute-start(bf16[4,128,1280]{2,1,0:T(8,128)(2,1)} %get-tuple-element.19), channel_id=1, source_target_pairs={{0,3},{1,2},{2,1},{3,0},{4,7},{5,6},{6,5},{7,4},{8,11},{9,10},{10,... | collective-permute-start | bytes 3932168 | tf_op jit(solution)/shard_map/ppermute | solution.py:280
  148.0 2.3 copy-start.14
  148.0 2.3 copy-start.15
  149.2 1.1 copy-start.1
  150.3 1.0 copy-start.9
  151.2 0.9 copy-start.10
  152.2 0.9 copy-start.11
  153.1 0.9 copy-start.12
  154.1 44.0 %copy-start.7 = (f32[512,128]{1,0:T(8,128)S(1)}, f32[512,128]{1,0:T(8,128)}, u32[]{:S(2)}) copy-start(f32[512,128]{1,0:T(8,128)} %pad_maximum_fusion.rest_0_) | copy-start | bytes 786436
  154.1 44.0 %copy-start.8 = (f32[512,128]{1,0:T(8,128)S(1)}, f32[512,128]{1,0:T(8,128)}, u32[]{:S(2)}) copy-start(f32[512,128]{1,0:T(8,128)} %pad_maximum_fusion.2.rest_2_) | copy-start | bytes 786436
  176.7 1.1 copy-start.16
  198.1 1.3 copy-start.2
  199.4 1.3 copy-start.3
  223.4 1.1 copy-start.4
  224.5 7.9 %copy-start.18 = (f32[4,20,64]{2,1,0:T(8,128)S(1)}, f32[4,20,64]{2,1,0:T(8,128)}, u32[]{:S(2)}) copy-start(f32[4,20,64]{2,1,0:T(8,128)} %get-tuple-element.34) | copy-start | bytes 61444
  224.5 78.6 %all-to-all-start.1 = ((bf16[32,8,2560]{2,1,0:T(8,128)(2,1)}), bf16[32,8,2560]{2,1,0:T(8,128)(2,1)S(1)}, u32[]{:S(2)}, u32[]{:S(2)}) async-start(bf16[32,8,2560]{2,1,0:T(8,128)(2,1)} %bitcast.36), calls=%async_computation.1 | async-start | bytes 2621440 | tf_op jit(solution)/shard_map/all_to_all | solution.py:424
  230.4 3.3 %collective-permute-start.3 = (bf16[4,128,1280]{2,1,0:T(8,128)(2,1)}, bf16[4,128,1280]{2,1,0:T(8,128)(2,1)S(1)}, u32[]{:S(2)}, u32[]{:S(2)}) collective-permute-start(bf16[4,128,1280]{2,1,0:T(8,128)(2,1)} %copy-done.16), channel_id=1, source_target_pairs={{0,1},{1,0},{2,3},{3,2},{4,5},{5,4},{6,7},{7,6},{8,9},{9,8},{10,11... | collective-permute-start | bytes 3932168 | tf_op jit(solution)/shard_map/ppermute | solution.py:280
  230.7 45.2 %collective-permute-start.4 = (bf16[4,128,1280]{2,1,0:T(8,128)(2,1)}, bf16[4,128,1280]{2,1,0:T(8,128)(2,1)S(1)}, u32[]{:S(2)}, u32[]{:S(2)}) collective-permute-start(bf16[4,128,1280]{2,1,0:T(8,128)(2,1)} %get-tuple-element.24), channel_id=1, source_target_pairs={{0,2},{1,3},{2,0},{3,1},{4,6},{5,7},{6,4},{7,5},{8,10},{9,11},{10,... | collective-permute-start | bytes 3932168 | tf_op jit(solution)/shard_map/ppermute | solution.py:280
  232.4 70.7 %collective-permute-start.5 = (bf16[4,128,1280]{2,1,0:T(8,128)(2,1)}, bf16[4,128,1280]{2,1,0:T(8,128)(2,1)}, u32[]{:S(2)}, u32[]{:S(2)}) collective-permute-start(bf16[4,128,1280]{2,1,0:T(8,128)(2,1)} %get-tuple-element.25), channel_id=1, source_target_pairs={{0,3},{1,2},{2,1},{3,0},{4,7},{5,6},{6,5},{7,4},{8,11},{9,10},{10,... | collective-permute-start | bytes 3932168 | tf_op jit(solution)/shard_map/ppermute | solution.py:280
  233.7 1.1 copy-start.5
  275.8 1.1 copy-start.17
  303.1 1.3 copy-start.6
where the time goes:
time: 311 us
  Pallas kernels  175 us (56%)
  waiting for transfers between devices  88.7 us (29%)
  starting transfers between devices  17.2 us (6%)
  local copies, waits for them, and re-layouts  16.7 us (5%)
  other arithmetic  12.2 us (4%)
    pallas_call x1, Pallas kernels, local(): pl.pallas_call(functools.partial(pack_kernel, blocks, edge), in_specs=[sm...  121 us
    ppermute x6, waiting for transfers between devices, swap(): return lax.ppermute(array, 'bal', [(i, i ^ k) for i in range(bal_size)])  88.7 us
    pallas_call x2, Pallas kernels, local(): pl.pallas_call(functools.partial(attend_kernel, per_step, blocks, count,...  45.2 us
    unnamed x44, local copies, waits for them, and re-layouts  15.5 us
    all_to_all x1, starting transfers between devices, local(): lax.all_to_all(jnp.broadcast_to(own_far[None], (devices, 2 * blocks, widt...  7.3 us
  transfers between devices with their start and end apart: 8, of which 4 were waited for; matrix products, arithmetic and copies ran while one was open for 3% of the time, Pallas kernels for 46%

commit v1 on v0

--- a/solution.py
+++ b/solution.py
@@ -166,19 +166,25 @@
 
 def pack_kernel(blocks, width, info, far_ref, *rest):
     inputs = rest[:4]
-    outs = rest[4 : 4 + blocks - 1]
-    sems = rest[4 + blocks - 1]
-    for wait in (False, True):
-        for k in reversed(range(1, blocks)):
-            rows = pl.ds(pl.multiple_of(info[k] * BLOCK, BLOCK), BLOCK)
-            for t in range(4):
-                move = pltpu.make_async_copy(
-                    inputs[t].at[rows, pl.ds(0, width)], outs[k - 1].at[t], sems.at[k - 1, t]
-                )
-                if wait:
-                    move.wait()
-                else:
-                    move.start()
+    outs = rest[4 : 3 + blocks]
+    room, load, save = rest[3 + blocks :]
+    order = [(k, t) for k in reversed(range(1, blocks)) for t in range(4)]
+
+    def pull(k, t):
+        rows = pl.ds(pl.multiple_of(info[k] * BLOCK, BLOCK), BLOCK)
+        source = inputs[t].at[rows, pl.ds(0, width)]
+        return pltpu.make_async_copy(source, room.at[k - 1, t], load.at[k - 1, t])
+
+    def push(k, t):
+        return pltpu.make_async_copy(room.at[k - 1, t], outs[k - 1].at[t], save.at[k - 1, t])
+
+    for k, t in order:
+        pull(k, t).start()
+    for k, t in order:
+        pull(k, t).wait()
+        push(k, t).start()
+    for k, t in order:
+        push(k, t).wait()
 
 
 def finish_kernel(heads, blocks, first, phase, slot, got_ref, cos_ref, sin_ref, *rest):
@@ -268,10 +274,11 @@
     assert blocks == bal_size and bal_size & (bal_size - 1) == 0
     bal = lax.axis_index("bal")
     device = lax.axis_index("ctx") * bal_size + bal
-    big = pltpu.CompilerParams(vmem_limit_bytes=50 * 1024 * 1024)
+    big = pltpu.CompilerParams(vmem_limit_bytes=60 * 1024 * 1024)
     smem = pl.BlockSpec(memory_space=pltpu.SMEM)
     vmem = pl.BlockSpec(memory_space=pltpu.VMEM)
     anywhere = pl.BlockSpec(memory_space=pl.ANY)
+    heavy = pl.CostEstimate(flops=20_000_000_000, bytes_accessed=60_000_000, transcendentals=0)
 
     def tokens_of(ids):
         return (ids[:, None] * BLOCK + jnp.arange(BLOCK, dtype=jnp.int32)[None, :]).reshape(rows)
@@ -329,7 +336,11 @@
         in_specs=[smem] + [anywhere] * 5,
         out_specs=[anywhere] * (blocks - 1),
         out_shape=[jax.ShapeDtypeStruct((4, BLOCK, edge), jnp.bfloat16)] * (blocks - 1),
-        scratch_shapes=[pltpu.SemaphoreType.DMA((blocks - 1, 4))],
+        scratch_shapes=[
+            pltpu.VMEM((blocks - 1, 4, BLOCK, edge), jnp.bfloat16),
+            pltpu.SemaphoreType.DMA((blocks - 1, 4)),
+            pltpu.SemaphoreType.DMA((blocks - 1, 4)),
+        ],
         compiler_params=big,
     )(info, own_far, queries, keys, values, output_gradient)
     come = [swap(sent[k - 1], k) for k in range(1, blocks)]
@@ -373,6 +384,7 @@
         out_shape=[jax.ShapeDtypeStruct((4, BLOCK, last * HEAD), jnp.bfloat16)] * blocks
         + [jax.ShapeDtypeStruct((side, width), jnp.bfloat16)],
         compiler_params=big,
+        cost_estimate=heavy,
     )(info, dilation_phase, segment_device_count, far, pull, push, cq, sq, ck, sk, *originals)
     parts, payload = list(results[:blocks]), results[blocks]
     for k in range(1, blocks):
@@ -405,6 +417,7 @@
         + [jax.ShapeDtypeStruct((side, width), jnp.bfloat16)],
         input_output_aliases={3 + 3 + 4 + 4 + blocks - 1: 4},
         compiler_params=big,
+        cost_estimate=heavy,
     )(
         moved,
         dilation_phase,

time: 311 us -> 202 us (0.65)
  Pallas kernels: 175 us -> 61.2 us
  waiting for transfers between devices: 88.7 us -> 99.7 us
  local copies, waits for them, and re-layouts: 16.7 us -> 8.01 us
  other arithmetic: 12.2 us -> 15.6 us
    pallas_call x1, Pallas kernels: 121 us -> 4.14 us  [local(): pl.pallas_call(functools.partial(pack_kernel, blocks, edge), in_specs=[sm...]
    all_to_all x1, waiting for transfers between devices: 0.01 us -> 14.5 us  [local(): lax.all_to_all(jnp.broadcast_to(own_far[None], (devices, 2 * blocks, widt...]
    unnamed x44 -> x20, local copies, waits for them, and re-layouts: 15.5 us -> 6.87 us
    ppermute x6, waiting for transfers between devices: 88.7 us -> 85.3 us  [swap(): return lax.ppermute(array, 'bal', [(i, i ^ k) for i in range(bal_size)])]
  transfers between devices with their start and end apart: 8 -> 8, of which waited for: 4 -> 4; matrix products, arithmetic and copies ran while one was open for 3% -> 6% of each run, Pallas kernels for 46% -> 13%
where the time goes in v1:
time: 202 us; the launch traced here: 201 us
  waiting for transfers between devices  99.7 us (49%)
  Pallas kernels  61.2 us (30%)
  starting transfers between devices  15.8 us (8%)
  other arithmetic  15.6 us (8%)
  local copies, waits for them, and re-layouts  8.01 us (4%)
    ppermute x6, waiting for transfers between devices, swap(): return lax.ppermute(array, 'bal', [(i, i ^ k) for i in range(bal_size)])  85.3 us
    pallas_call x2, Pallas kernels, local(): pl.pallas_call(functools.partial(attend_kernel, per_step, blocks, count,...  45.3 us
    all_to_all x1, waiting for transfers between devices, local(): lax.all_to_all(jnp.broadcast_to(own_far[None], (devices, 2 * blocks, widt...  14.5 us
    pallas_call x1, Pallas kernels, local(): pl.pallas_call(functools.partial(finish_kernel, heads, blocks, first), in...  7.6 us
    all_to_all x1, starting transfers between devices, local(): lax.all_to_all(jnp.broadcast_to(own_far[None], (devices, 2 * blocks, widt...  7.3 us
    unnamed x20, local copies, waits for them, and re-layouts  6.87 us
    all_to_all x1, starting transfers between devices, local(): lax.all_to_all(payload.reshape(devices, 2 * blocks, width), ('ctx', 'bal'...  4.53 us
    pallas_call x1, Pallas kernels, local(): pl.pallas_call(functools.partial(pick_kernel, heads, blocks), in_specs=[s...  4.17 us
  transfers between devices with their start and end apart: 8, of which 4 were waited for; matrix products, arithmetic and copies ran while one was open for 6% of the time, Pallas kernels for 13%

profile of v1, /device:TPU:0, one launch (start us, length us, event | category | flops | bytes accessed | tf_op | source)
XLA Modules:
  0.0 201.1 jit_solution(17190015937998803687)
XLA Ops:
  0.7 0.8 select_reduce_fusion.1
  1.5 0.7 add_multiply_fusion
  2.3 0.7 add_convert_fusion
  4.9 4.2 %shard_map.102 = f32[8,2560]{1,0:T(8,128)} custom-call(s32[20]{0:T(128)} %phase.7, bf16[512,2560]{1,0:T(8,128)(2,1)} %rest_5_.3, bf16[512,2560]{1,0:T(8,128)(2,1)} %rest_6_.3, f32[4,2560]{1,0:T(4,128)} %bitcast.43, f32[4,2560]{1,0:T(4,128)} %bitcast.44), custom_call_target="tpu_custom_call" | custom-call | tf_op jit(solution)/shard_map/pallas_call | solution.py:305
  9.0 0.9 convert_element_type.58.far_ref
  9.9 1.1 broadcast_in_dim.41
  11.1 7.3 %all-to-all-start = ((bf16[32,8,2560]{2,1,0:T(8,128)(2,1)}), bf16[32,8,2560]{2,1,0:T(8,128)(2,1)S(1)}, u32[]{:S(2)}, u32[]{:S(2)}) async-start(bf16[32,8,2560]{2,1,0:T(8,128)(2,1)} %broadcast_in_dim.41), calls=%async_computation | async-start | bytes 2621440 | tf_op jit(solution)/shard_map/all_to_all | solution.py:323
  19.3 4.1 %shard_map.103 = (bf16[4,128,1280]{2,1,0:T(8,128)(2,1)}, bf16[4,128,1280]{2,1,0:T(8,128)(2,1)}, bf16[4,128,1280]{2,1,0:T(8,128)(2,1)}) custom-call(s32[8]{0:T(128)} %pad_add_fusion.2.info, bf16[8,2560]{1,0:T(8,128)(2,1)} %copy-done.4, bf16[512,2560]{1,0:T(8,128)(2,1)} %rest_4_.3, bf16[512,2560]{1,0:T(8,128)(2,1)} %rest_5_.3, bf16[512,2560]{1,0:T(8,128)(2,1)} %rest_6_.3, ...), custom_call_target="tpu_custom_call" | custom-call | tf_op jit(solution)/shard_map/pallas_call | solution.py:334
  23.8 1.7 collective-permute-start.1
  26.6 2.1 %fusion.13 = (f32[512,64]{1,0:T(8,128)S(1)}, f32[512,64]{1,0:T(8,128)S(1)}, f32[512,64]{1,0:T(8,128)S(1)}, f32[512,64]{1,0:T(8,128)S(1)}, f32[512,64]{1,0:T(8,12...) fusion(f32[64]{0:T(128)S(1)} %get-tuple-element.67, ...), kind=kLoop, calls=%fused_computation.33 | loop fusion | flops 589824 | bytes 1581568 | tf_op jit(solution)/shard_map/neg | solution.py:32
  28.7 0.8 pad_maximum_fusion.4.rest_0_
  29.5 0.8 pad_maximum_fusion.6.rest_2_
  30.3 0.8 pad_maximum_fusion.rest_0_
  31.2 0.8 pad_maximum_fusion.2.rest_2_
  32.0 0.8 pad_maximum_fusion.7.rest_3_
  32.8 0.8 pad_maximum_fusion.5.rest_1_
  33.7 0.9 pad_maximum_fusion.3.rest_3_
  34.6 0.9 pad_maximum_fusion.1.rest_1_
  35.4 0.8 fusion.10
  36.2 14.5 %all-to-all-done = bf16[32,8,2560]{2,1,0:T(8,128)(2,1)S(1)} async-done(((bf16[32,8,2560]{2,1,0:T(8,128)(2,1)}), bf16[32,8,2560]{2,1,0:T(8,128)(2,1)S(1)}, u32[]{:S(2)}, u32[]{:S(2)}) %all-to-all-start) | async-done | bytes 1310752 | tf_op jit(solution)/shard_map/all_to_all | solution.py:323
  50.6 1.1 copy-done.3
  51.8 22.6 %shard_map.104 = (bf16[4,128,1280]{2,1,0:T(8,128)(2,1)}, bf16[4,128,1280]{2,1,0:T(8,128)(2,1)}, bf16[4,128,1280]{2,1,0:T(8,128)(2,1)}, bf16[4,128,1280]{2,1,0:T(8,128)(2,1)}, bf16[256,2560]{1,0:T(8,128)(2,1)}) custom-call(s32[8]{0:T(128)} %pad_add_fusion.2.info, s32[20]{0:T(128)} %phase.7, s32[20]{0:T(128)} %seg.3, bf16[256,2560]{1,0:T(8,128)(2,1)} %bitcast.38, ...), custom_call_target="tpu_custom_call" | custom-call | flops 20000000000 | bytes 60000000 | tf_op jit(solution)/shard_map/pallas_call | solution.py:375
  74.4 17.1 %collective-permute-done.2.rest_10_ = bf16[4,128,1280]{2,1,0:T(8,128)(2,1)S(1)} collective-permute-done((bf16[4,128,1280]{2,1,0:T(8,128)(2,1)}, bf16[4,128,1280]{2,1,0:T(8,128)(2,1)S(1)}, u32[]{:S(2)}, u32[]{:S(2)}) %collective-permute-start.2) | collective-permute-done | bytes 1310752 | tf_op jit(solution)/shard_map/ppermute | solution.py:287
  91.5 1.1 copy-done.6
  92.5 22.7 %shard_map.105 = (bf16[4,128,2560]{2,1,0:T(8,128)(2,1)}, bf16[4,128,2560]{2,1,0:T(8,128)(2,1)}, bf16[4,128,2560]{2,1,0:T(8,128)(2,1)}, bf16[4,128,2560]{2,1,0:T(8,128)(2,1)}, bf16[256,2560]{1,0:T(8,128)(2,1)}) custom-call(s32[12]{0:T(128)} %pad_add_fusion.1.info, s32[20]{0:T(128)} %phase.7, s32[20]{0:T(128)} %seg.3, ...), custom_call_target="tpu_custom_call", output_to_operand_aliasing={{4}: (17, {})} | custom-call | flops 20000000000 | bytes 60000000 | tf_op jit(solution)/shard_map/pallas_call | solution.py:403
  115.2 4.5 %all-to-all-start.1 = ((bf16[32,8,2560]{2,1,0:T(8,128)(2,1)}), bf16[32,8,2560]{2,1,0:T(8,128)(2,1)S(1)}, u32[]{:S(2)}, u32[]{:S(2)}) async-start(bf16[32,8,2560]{2,1,0:T(8,128)(2,1)} %bitcast.40), calls=%async_computation.1 | async-start | bytes 2621440 | tf_op jit(solution)/shard_map/all_to_all | solution.py:437
  120.1 1.7 collective-permute-start.4
  123.2 42.0 %collective-permute-done.4.rest_2_ = bf16[4,128,1280]{2,1,0:T(8,128)(2,1)S(1)} collective-permute-done((bf16[4,128,1280]{2,1,0:T(8,128)(2,1)}, bf16[4,128,1280]{2,1,0:T(8,128)(2,1)S(1)}, u32[]{:S(2)}, u32[]{:S(2)}) %collective-permute-start.4) | collective-permute-done | bytes 1310752 | tf_op jit(solution)/shard_map/ppermute | solution.py:287
  165.2 1.1 copy-done.2
  166.3 26.2 %collective-permute-done.5.rest_3_ = bf16[4,128,1280]{2,1,0:T(8,128)(2,1)} collective-permute-done((bf16[4,128,1280]{2,1,0:T(8,128)(2,1)}, bf16[4,128,1280]{2,1,0:T(8,128)(2,1)}, u32[]{:S(2)}, u32[]{:S(2)}) %collective-permute-start.5) | collective-permute-done | bytes 1310752 | tf_op jit(solution)/shard_map/ppermute | solution.py:287
  192.5 1.1 copy-done
  193.5 7.6 %shard_map.106 = (bf16[512,2560]{1,0:T(8,128)(2,1)}, bf16[512,2560]{1,0:T(8,128)(2,1)}, bf16[512,2560]{1,0:T(8,128)(2,1)}, bf16[512,2560]{1,0:T(8,128)(2,1)}) custom-call(s32[20]{0:T(128)} %phase.7, s32[4]{0:T(128)} %copy-done.5, bf16[32,8,2560]{2,1,0:T(8,128)(2,1)} %copy-done, ...), custom_call_target="tpu_custom_call", output_to_operand_aliasing={{0}: (9, {}), {1}: (10, {}), {2}: (11, {}), {3}: (12, {})} | custom-call | tf_op jit(solution)/shard_map/pallas_call | solution.py:448
  (48 shorter events, 6.0 us)
Async XLA Ops:
  9.9 1.1 copy-start.4
  11.1 7.3 %copy-start.7 = (s32[128]{0:T(128)S(1)}, s32[128]{0:T(128)}, u32[]{:S(2)}) copy-start(s32[128]{0:T(128)} %param.13) | copy-start | bytes 1540
  11.1 39.5 %all-to-all-start = ((bf16[32,8,2560]{2,1,0:T(8,128)(2,1)}), bf16[32,8,2560]{2,1,0:T(8,128)(2,1)S(1)}, u32[]{:S(2)}, u32[]{:S(2)}) async-start(bf16[32,8,2560]{2,1,0:T(8,128)(2,1)} %broadcast_in_dim.41), calls=%async_computation | async-start | bytes 2621440 | tf_op jit(solution)/shard_map/all_to_all | solution.py:323
  18.4 7.3 %copy-start.5 = (s32[4]{0:T(128)}, s32[4]{0:T(128)S(1)}, u32[]{:S(2)}) copy-start(s32[4]{0:T(128)S(1)} %iota_xor_fusion.slot) | copy-start | bytes 52
  23.5 50.9 %collective-permute-start = (bf16[4,128,1280]{2,1,0:T(8,128)(2,1)}, bf16[4,128,1280]{2,1,0:T(8,128)(2,1)}, u32[]{:S(2)}, u32[]{:S(2)}) collective-permute-start(bf16[4,128,1280]{2,1,0:T(8,128)(2,1)} %get-tuple-element.17), channel_id=1, source_target_pairs={{0,1},{1,0},{2,3},{3,2},{4,5},{5,4},{6,7},{7,6},{8,9},{9,8},{10,11... | collective-permute-start | bytes 3932168 | tf_op jit(solution)/shard_map/ppermute | solution.py:287
  23.8 50.6 %collective-permute-start.1 = (bf16[4,128,1280]{2,1,0:T(8,128)(2,1)}, bf16[4,128,1280]{2,1,0:T(8,128)(2,1)}, u32[]{:S(2)}, u32[]{:S(2)}) collective-permute-start(bf16[4,128,1280]{2,1,0:T(8,128)(2,1)} %get-tuple-element.18), channel_id=1, source_target_pairs={{0,2},{1,3},{2,0},{3,1},{4,6},{5,7},{6,4},{7,5},{8,10},{9,11},{10,... | collective-permute-start | bytes 3932168 | tf_op jit(solution)/shard_map/ppermute | solution.py:287
  25.5 66.0 %collective-permute-start.2 = (bf16[4,128,1280]{2,1,0:T(8,128)(2,1)}, bf16[4,128,1280]{2,1,0:T(8,128)(2,1)S(1)}, u32[]{:S(2)}, u32[]{:S(2)}) collective-permute-start(bf16[4,128,1280]{2,1,0:T(8,128)(2,1)} %get-tuple-element.19), channel_id=1, source_target_pairs={{0,3},{1,2},{2,1},{3,0},{4,7},{5,6},{6,5},{7,4},{8,11},{9,10},{10,... | collective-permute-start | bytes 3932168 | tf_op jit(solution)/shard_map/ppermute | solution.py:287
  50.6 1.1 copy-start.3
  91.4 1.1 copy-start.6
  115.2 77.2 %all-to-all-start.1 = ((bf16[32,8,2560]{2,1,0:T(8,128)(2,1)}), bf16[32,8,2560]{2,1,0:T(8,128)(2,1)S(1)}, u32[]{:S(2)}, u32[]{:S(2)}) async-start(bf16[32,8,2560]{2,1,0:T(8,128)(2,1)} %bitcast.40), calls=%async_computation.1 | async-start | bytes 2621440 | tf_op jit(solution)/shard_map/all_to_all | solution.py:437
  119.8 3.4 %collective-permute-start.3 = (bf16[4,128,1280]{2,1,0:T(8,128)(2,1)}, bf16[4,128,1280]{2,1,0:T(8,128)(2,1)S(1)}, u32[]{:S(2)}, u32[]{:S(2)}) collective-permute-start(bf16[4,128,1280]{2,1,0:T(8,128)(2,1)} %get-tuple-element.23), channel_id=1, source_target_pairs={{0,1},{1,0},{2,3},{3,2},{4,5},{5,4},{6,7},{7,6},{8,9},{9,8},{10,11... | collective-permute-start | bytes 3932168 | tf_op jit(solution)/shard_map/ppermute | solution.py:287
  120.1 45.2 %collective-permute-start.4 = (bf16[4,128,1280]{2,1,0:T(8,128)(2,1)}, bf16[4,128,1280]{2,1,0:T(8,128)(2,1)S(1)}, u32[]{:S(2)}, u32[]{:S(2)}) collective-permute-start(bf16[4,128,1280]{2,1,0:T(8,128)(2,1)} %get-tuple-element.24), channel_id=1, source_target_pairs={{0,2},{1,3},{2,0},{3,1},{4,6},{5,7},{6,4},{7,5},{8,10},{9,11},{10,... | collective-permute-start | bytes 3932168 | tf_op jit(solution)/shard_map/ppermute | solution.py:287
  121.8 70.7 %collective-permute-start.5 = (bf16[4,128,1280]{2,1,0:T(8,128)(2,1)}, bf16[4,128,1280]{2,1,0:T(8,128)(2,1)}, u32[]{:S(2)}, u32[]{:S(2)}) collective-permute-start(bf16[4,128,1280]{2,1,0:T(8,128)(2,1)} %get-tuple-element.25), channel_id=1, source_target_pairs={{0,3},{1,2},{2,1},{3,0},{4,7},{5,6},{6,5},{7,4},{8,11},{9,10},{10,... | collective-permute-start | bytes 3932168 | tf_op jit(solution)/shard_map/ppermute | solution.py:287
  123.2 69.3 %copy-start.1 = (bf16[4,128,1280]{2,1,0:T(8,128)(2,1)}, bf16[4,128,1280]{2,1,0:T(8,128)(2,1)S(1)}, u32[]{:S(2)}) copy-start(bf16[4,128,1280]{2,1,0:T(8,128)(2,1)S(1)} %collective-permute-done.3.rest_1_) | copy-start | bytes 3932164
  165.2 1.1 copy-start.2
  192.5 1.1 copy-start

commit v2 on v0

v2 whole, which is shorter than its diff:
```python
import functools
import math

import jax
import jax.numpy as jnp
from jax import lax
from jax.experimental import pallas as pl
from jax.experimental.pallas import tpu as pltpu
from jax.sharding import PartitionSpec as P

BLOCK = 128
HEAD = 128
LOG2E = 1.4426950408889634
NT = (((1,), (1,)), ((), ()))
TN = (((0,), (0,)), ((), ()))


def tables(positions, total):
    half = HEAD // 2
    pair = jnp.arange(half, dtype=jnp.float32)
    inverse = jnp.exp(pair * (-2.0 * math.log(10000.0) / HEAD))
    where = positions.astype(jnp.float32)[..., None]
    angles = where * inverse
    base = (2.0 * pair / HEAD + 0.4) / 1.4
    growth = jnp.exp((2.0 * where - total) / total * jnp.log(base))
    cosine, sine = jnp.cos(angles), jnp.sin(angles)

    def pack(scale):
        first, second = cosine * scale, sine * scale
        return (
            jnp.concatenate([first, first], axis=-1),
            jnp.concatenate([-second, second], axis=-1),
        )

    return pack(growth) + pack(1.0 / growth)


def dot(left, right, dims=None):
    if dims is None:
        dims = (((1,), (0,)), ((), ()))
    return lax.dot_general(left, right, dims, preferred_element_type=jnp.float32)


def attend_kernel(
    per_step, blocks, count, first, relaid, info, phase, seg, far_ref, pull_ref, push_ref, *rest
):
    cq_ref, sq_ref, ck_ref, sk_ref = rest[:4]
    own = rest[4:8]
    rest = rest[8:]
    if relaid:
        come, rest = rest[: blocks - 1], rest[blocks - 1 + relaid :]
        finals, rest = rest[:4], rest[4:]
    else:
        finals, rest = rest[:blocks], rest[blocks:]
    pay_ref, near_k, near_v, far_sum = rest
    scale = 1.0 / math.sqrt(HEAD)
    key_at = lax.broadcasted_iota(jnp.int32, (BLOCK, BLOCK), 0)
    query_at = lax.broadcasted_iota(jnp.int32, (BLOCK, BLOCK), 1)
    causal = key_at <= query_at
    far_at = lax.broadcasted_iota(jnp.int32, (count, BLOCK), 0)
    half = HEAD // 2
    for sub in range(per_step):
        head = first + pl.program_id(0) * per_step + sub
        lanes = slice(sub * HEAD, (sub + 1) * HEAD)
        both = dot(pull_ref[...], far_ref[:, lanes]).astype(jnp.bfloat16)
        far_k, far_v = both[:count], both[count:]
        span = seg[head] * blocks
        p_far, d_far, q_all, g_all = [], [], [], []
        for k in range(blocks):
            if relaid:
                rows = slice(k * BLOCK, (k + 1) * BLOCK)
                source = [ref[:, lanes] for ref in own]
                if k:
                    source = [come[k - 1][t, :, lanes] for t in range(4)]
            else:
                rows = pl.ds(pl.multiple_of(info[k] * BLOCK, BLOCK), BLOCK)
                source = [ref[rows, lanes] for ref in own]
            block = info[blocks + k]
            low = block & (-span)
            cq, sq, ck, sk = cq_ref[rows, :], sq_ref[rows, :], ck_ref[rows, :], sk_ref[rows, :]
            raw_q, raw_k, value, grad = source
            raw_q = raw_q.astype(jnp.float32)
            raw_k = raw_k.astype(jnp.float32)
            tq = (raw_q * cq + pltpu.roll(raw_q, half, 1) * sq).astype(jnp.bfloat16)
            tk = (raw_k * ck + pltpu.roll(raw_k, half, 1) * sk).astype(jnp.bfloat16)
            keys = jnp.concatenate([tk, far_k], axis=0)
            vals = jnp.concatenate([value, far_v], axis=0)
            score = dot(keys, tq, NT)
            allowed = (far_at >= low) & (far_at < block)
            score = jnp.concatenate(
                [
                    jnp.where(causal, score[:BLOCK], -jnp.inf),
                    jnp.where(allowed, score[BLOCK:], -jnp.inf),
                ],
                axis=0,
            )
            top = jnp.max(score, axis=0, keepdims=True)
            weight = jnp.exp2((score - top) * (scale * LOG2E))
            prob = weight * (1.0 / jnp.sum(weight, axis=0, keepdims=True))
            p16 = prob.astype(jnp.bfloat16)
            dprob = dot(vals, grad, NT)
            delta = jnp.sum(p16.astype(jnp.float32) * dprob, axis=0, keepdims=True)
            d16 = (prob * (dprob - delta)).astype(jnp.bfloat16)
            out = dot(p16, vals, TN)
            dq = dot(d16, keys, TN) * scale
            dk = dot(d16[:BLOCK], tq) * scale
            dv = dot(p16[:BLOCK], grad)
            near_k[k] = dk
            near_v[k] = dv
            made = (
                out,
                dq * cq - pltpu.roll(dq, half, 1) * sq,
                dk * ck - pltpu.roll(dk, half, 1) * sk,
                dv,
            )
            for t in range(4):
                if relaid:
                    finals[t][info[2 * blocks + k], :, lanes] = made[t].astype(jnp.bfloat16)
                else:
                    finals[k][t, :, lanes] = made[t].astype(jnp.bfloat16)
            p_far.append(p16[BLOCK:])
            d_far.append(d16[BLOCK:])
            q_all.append(tq)
            g_all.append(grad)
        far_sum[:count] = (
            dot(jnp.concatenate(d_far, axis=1), jnp.concatenate(q_all, axis=0)) * scale
        )
        far_sum[count:] = dot(jnp.concatenate(p_far, axis=1), jnp.concatenate(g_all, axis=0))
        at = phase[head]
        for k in range(blocks):
            block = info[blocks + k]
            far_sum[pl.ds(block, 1), :] = far_sum[pl.ds(block, 1), :] + near_k[k, pl.ds(at, 1), :]
            far_sum[pl.ds(count + block, 1), :] = (
                far_sum[pl.ds(count + block, 1), :] + near_v[k, pl.ds(at, 1), :]
            )
        pay_ref[:, lanes] = dot(push_ref[...], far_sum[...].astype(jnp.bfloat16)).astype(
            jnp.bfloat16
        )


def pick_kernel(
    heads, blocks, phase, k_hbm, v_hbm, cos_ref, sin_ref, after, out_ref, k_ref, v_ref, row_ref,
    load, save
):
    moves = [
        pltpu.make_async_copy(k_hbm, k_ref, load.at[0]),
        pltpu.make_async_copy(v_hbm, v_ref, load.at[1]),
    ]
    for move in moves:
        move.start()
    for move in moves:
        move.wait()
    spot = lax.broadcasted_iota(jnp.int32, (16, HEAD), 0)
    for head in range(heads):
        at = phase[head]
        start = pl.multiple_of(at // 16 * 16, 16)
        lanes = slice(head * HEAD, (head + 1) * HEAD)
        both = []
        for ref in (k_ref, v_ref):
            rows = []
            for k in range(blocks):
                tile = ref[pl.ds(pl.multiple_of(k * BLOCK + start, 16), 16), lanes]
                tile = jnp.where(spot == at - start, tile.astype(jnp.float32), 0.0)
                rows.append(jnp.sum(tile, axis=0, keepdims=True))
            both.append(jnp.concatenate(rows, axis=0))
        key, value = both
        key = key * cos_ref[:, lanes] + pltpu.roll(key, HEAD // 2, 1) * sin_ref[:, lanes]
        row_ref[:, lanes] = jnp.concatenate([key, value], axis=0).astype(jnp.bfloat16)
    copies = [
        pltpu.make_async_copy(row_ref, out_ref.at[d], save.at[d]) for d in range(out_ref.shape[0])
    ]
    for copy in copies:
        copy.start()
    for copy in copies:
        copy.wait()


def pack_kernel(jobs, info, after, *rest):
    number = len(jobs)
    inputs, rest = rest[:4], rest[4:]
    outs, rooms, (load, save) = rest[:number], rest[number : 2 * number], rest[2 * number :]
    order = [(job, t) for job in range(number) for t in range(4)]

    def fetch(job, t):
        k, start, width = jobs[job]
        rows = pl.ds(pl.multiple_of(info[k] * BLOCK, BLOCK), BLOCK)
        source = inputs[t].at[rows, pl.ds(start, width)]
        return pltpu.make_async_copy(source, rooms[job].at[t], load.at[job, t])

    def store(job, t):
        return pltpu.make_async_copy(rooms[job].at[t], outs[job].at[t], save.at[job, t])

    for job, t in order:
        fetch(job, t).start()
    for job, t in order:
        fetch(job, t).wait()
        store(job, t).start()
    for job, t in order:
        store(job, t).wait()


def place_kernel(blocks, edge, slot, *rest):
    parts = rest[:blocks]
    finals = rest[blocks + 4 : blocks + 8]
    room, load, save = rest[blocks + 8 :]
    width = room.shape[-1]

    def save_of(k, t):
        where = finals[t].at[pl.ds(k * BLOCK, BLOCK), pl.ds(edge, width)]
        return pltpu.make_async_copy(room.at[k, t], where, save.at[k, t])

    loads = [pltpu.make_async_copy(parts[k], room.at[slot[k]], load.at[k]) for k in range(blocks)]
    for move in loads:
        move.start()
    for move in loads:
        move.wait()
    for k in range(blocks):
        for t in range(4):
            save_of(k, t).start()
    for k in range(blocks):
        for t in range(4):
            save_of(k, t).wait()


def patch_kernel(
    heads, blocks, phase, got_hbm, cos_ref, sin_ref, dk_in, dv_in, dk_out, dv_out, got, room, get,
    load, save
):
    def rows(k):
        return pl.ds(k * BLOCK, BLOCK)

    outs = (dk_out, dv_out)
    order = [(k, t) for k in range(blocks) for t in range(2)]
    fetch = pltpu.make_async_copy(got_hbm, got, get)
    loads = [pltpu.make_async_copy(outs[t].at[rows(k)], room.at[t, k], load.at[t, k]) for k, t in order]
    saves = [pltpu.make_async_copy(room.at[t, k], outs[t].at[rows(k)], save.at[t, k]) for k, t in order]
    fetch.start()
    for move in loads:
        move.start()
    fetch.wait()
    total = got[0].astype(jnp.float32)
    for sender in range(1, got.shape[0]):
        total = total + got[sender].astype(jnp.float32)
    far_k, far_v = total[:blocks], total[blocks:]
    spot = lax.broadcasted_iota(jnp.int32, (16, HEAD), 0)
    fresh = []
    for head in range(heads):
        lanes = slice(head * HEAD, (head + 1) * HEAD)
        turned = far_k[:, lanes] * cos_ref[:, lanes] - pltpu.roll(
            far_k[:, lanes], HEAD // 2, 1
        ) * sin_ref[:, lanes]
        fresh.append((turned, far_v[:, lanes]))
    for index, (k, t) in enumerate(order):
        loads[index].wait()
        for head in range(heads):
            at = phase[head]
            start = pl.multiple_of(at // 16 * 16, 16)
            lanes = slice(head * HEAD, (head + 1) * HEAD)
            old = room[t, k, pl.ds(start, 16), lanes].astype(jnp.float32)
            row = fresh[head][t][k : k + 1]
            room[t, k, pl.ds(start, 16), lanes] = jnp.where(spot == at - start, row, old).astype(
                jnp.bfloat16
            )
        saves[index].start()
    for move in saves:
        move.wait()


def local(queries, keys, values, output_gradient, dilation_phase, segment_device_count, owner):
    rows, width = queries.shape
    heads = width // HEAD
    blocks = rows // BLOCK
    bal_size = lax.axis_size("bal")
    devices = lax.axis_size("ctx") * bal_size
    total = rows * devices
    count = owner.shape[0]
    assert blocks == bal_size and bal_size & (bal_size - 1) == 0
    bal = lax.axis_index("bal")
    device = lax.axis_index("ctx") * bal_size + bal
    big = pltpu.CompilerParams(vmem_limit_bytes=60 * 1024 * 1024)
    smem = pl.BlockSpec(memory_space=pltpu.SMEM)
    vmem = pl.BlockSpec(memory_space=pltpu.VMEM)
    anywhere = pl.BlockSpec(memory_space=pl.ANY)
    light = pl.CostEstimate(flops=2_000_000_000, bytes_accessed=5_000_000, transcendentals=0)
    heavy = pl.CostEstimate(flops=20_000_000_000, bytes_accessed=60_000_000, transcendentals=0)
    huge = pl.CostEstimate(flops=1000, bytes_accessed=400_000_000, transcendentals=0)

    def tokens_of(ids):
        return (ids[:, None] * BLOCK + jnp.arange(BLOCK, dtype=jnp.int32)[None, :]).reshape(rows)

    def swap(array, k):
        return lax.ppermute(array, "bal", [(i, i ^ k) for i in range(bal_size)])

    steps = jnp.arange(blocks, dtype=jnp.int32)
    held = device * blocks + steps
    goes_to = lax.dynamic_slice_in_dim(owner, device * blocks, blocks) // blocks % bal_size
    partner = steps ^ bal
    which = jnp.sum(jnp.where(goes_to[None, :] == partner[:, None], steps[None, :], 0), axis=1)
    info = jnp.concatenate([which, device * blocks + which]).astype(jnp.int32)
    comes_from = jnp.sum(
        jnp.where(
            owner[None, :] == held[:, None], jnp.arange(count, dtype=jnp.int32)[None, :], 0
        ),
        axis=1,
    )

    first = heads // 4 * 2
    early = first // 4 * 2
    last = heads - first
    edge = first * HEAD
    originals = (queries, keys, values, output_gradient)

    def send_inputs(jobs, after):
        sizes = [(4, BLOCK, width) for _, _, width in jobs]
        sent = pl.pallas_call(
            functools.partial(pack_kernel, jobs),
            in_specs=[smem] + [anywhere] * 5,
            out_specs=[anywhere] * len(jobs),
            out_shape=[jax.ShapeDtypeStruct(size, jnp.bfloat16) for size in sizes],
            scratch_shapes=[pltpu.VMEM(size, jnp.bfloat16) for size in sizes]
            + [pltpu.SemaphoreType.DMA((len(jobs), 4))] * 2,
            compiler_params=big,
        )(info, after, *originals)
        return sent, [swap(one, job[0]) for one, job in zip(sent, jobs)]

    cut = early * HEAD
    across = range(2, blocks)
    sent, come_early = send_inputs([(k, 0, cut) for k in across], owner)

    cq, sq, ck, sk = tables(tokens_of(held), total)
    own_phase = (held[:, None] * BLOCK + dilation_phase[None, :]).astype(jnp.int32)
    _, _, pick_cos, pick_sin = tables(own_phase, total)
    own_far = pl.pallas_call(
        functools.partial(pick_kernel, heads, blocks),
        in_specs=[smem, anywhere, anywhere, vmem, vmem, anywhere],
        out_specs=anywhere,
        out_shape=jax.ShapeDtypeStruct((devices, 2 * blocks, width), jnp.bfloat16),
        scratch_shapes=[
            pltpu.VMEM((rows, width), jnp.bfloat16),
            pltpu.VMEM((rows, width), jnp.bfloat16),
            pltpu.VMEM((2 * blocks, width), jnp.bfloat16),
            pltpu.SemaphoreType.DMA((2,)),
            pltpu.SemaphoreType.DMA((devices,)),
        ],
        compiler_params=big,
    )(
        dilation_phase,
        keys,
        values,
        pick_cos.reshape(blocks, width),
        pick_sin.reshape(blocks, width),
        sent[0],
    )
    far = lax.all_to_all(
        own_far, ("ctx", "bal"), split_axis=0, concat_axis=0, tiled=True
    ).reshape(devices * 2 * blocks, width)
    _, come_late = send_inputs([(k, cut, edge - cut) for k in across] + [(1, 0, edge)], own_far)
    come_early = [come_late[-1]] + come_early
    come_late = [come_late[-1]] + come_late[:-1]

    side = 2 * count
    wide = jnp.arange(side, dtype=jnp.int32)
    tall = wide[:, None]
    wide = wide[None, :]
    source = tall % count
    pull = (
        wide == source // blocks * (2 * blocks) + tall // count * blocks + source % blocks
    ).astype(jnp.bfloat16)
    lands = owner // blocks * (2 * blocks) + owner % blocks
    push = (jnp.concatenate([lands, lands + blocks])[None, :] == tall).astype(jnp.bfloat16)

    per_step = 2
    columns = per_step * HEAD
    fixed = lambda h, *_: (0, 0)
    square = pl.BlockSpec((side, side), fixed)
    table = pl.BlockSpec((rows, HEAD), fixed)
    part = pl.BlockSpec((4, BLOCK, columns), lambda h, *_: (0, 0, h))
    scratch = [
        pltpu.VMEM((blocks, BLOCK, HEAD), jnp.float32),
        pltpu.VMEM((blocks, BLOCK, HEAD), jnp.float32),
        pltpu.VMEM((side, HEAD), jnp.float32),
    ]
    skip = first // per_step
    tensor = pl.BlockSpec((rows, columns), lambda h, *_: (0, h + skip))
    lane = pl.BlockSpec((side, columns), lambda h, *_: (0, h + skip))
    results = pl.pallas_call(
        functools.partial(attend_kernel, per_step, blocks, count, first, 0),
        grid_spec=pltpu.PrefetchScalarGridSpec(
            num_scalar_prefetch=3,
            grid=(last // per_step,),
            in_specs=[lane, square, square] + [table] * 4 + [tensor] * 4,
            out_specs=[part] * blocks + [lane],
            scratch_shapes=scratch,
        ),
        out_shape=[jax.ShapeDtypeStruct((4, BLOCK, last * HEAD), jnp.bfloat16)] * blocks
        + [jax.ShapeDtypeStruct((side, width), jnp.bfloat16)],
        compiler_params=big,
        cost_estimate=heavy,
    )(info, dilation_phase, segment_device_count, far, pull, push, cq, sq, ck, sk, *originals)
    parts, payload = list(results[:blocks]), results[blocks]
    for k in range(1, blocks):
        parts[k] = swap(parts[k], k)

    ids = (device ^ steps) * blocks
    came = jnp.sum(
        jnp.where(comes_from[None, :] // blocks * blocks == ids[:, None], comes_from[None, :], 0),
        axis=1,
    )
    moved = jnp.concatenate([which, came, partner]).astype(jnp.int32)
    cq, sq, ck, sk = tables(tokens_of(came), total)
    shapes = [jax.ShapeDtypeStruct((blocks, BLOCK, width), jnp.bfloat16)] * 4
    shapes = shapes + [jax.ShapeDtypeStruct((side, width), jnp.bfloat16)]

    def attend_relaid(begin, end, come, carried):
        skip = begin // per_step
        tensor = pl.BlockSpec((BLOCK, columns), lambda h, info, *_: (info[0], h + skip))
        lane = pl.BlockSpec((side, columns), lambda h, *_: (0, h + skip))
        whole = pl.BlockSpec((blocks, BLOCK, columns), lambda h, *_: (0, 0, h + skip))
        operands = 3 + 3 + 4 + 4 + blocks - 1
        return pl.pallas_call(
            functools.partial(attend_kernel, per_step, blocks, count, begin, len(carried)),
            grid_spec=pltpu.PrefetchScalarGridSpec(
                num_scalar_prefetch=3,
                grid=((end - begin) // per_step,),
                in_specs=[lane, square, square]
                + [table] * 4
                + [tensor] * 4
                + [pl.BlockSpec((4, BLOCK, columns), lambda h, *_: (0, 0, h + skip))]
                + [part] * (blocks - 2)
                + [anywhere] * len(carried),
                out_specs=[whole] * 4 + [lane],
                scratch_shapes=scratch,
            ),
            out_shape=shapes,
            input_output_aliases={
                operands + i: 5 - len(carried) + i for i in range(len(carried))
            },
            compiler_params=big,
            cost_estimate=light,
        )(
            moved,
            dilation_phase,
            segment_device_count,
            far,
            pull,
            push,
            cq,
            sq,
            ck,
            sk,
            *originals,
            *come,
            *carried,
        )

    results = attend_relaid(0, early, come_early, [payload])
    results = attend_relaid(early, first, come_late, results)
    finals, payload = [one.reshape(rows, width) for one in results[:4]], results[4]
    got = lax.all_to_all(
        payload.reshape(devices, 2 * blocks, width),
        ("ctx", "bal"),
        split_axis=0,
        concat_axis=0,
        tiled=True,
    )

    new_phase = (comes_from[:, None] * BLOCK + dilation_phase[None, :]).astype(jnp.int32)
    _, _, new_cos, new_sin = tables(new_phase, total)
    out = jax.ShapeDtypeStruct((rows, width), jnp.bfloat16)
    finals = pl.pallas_call(
        functools.partial(place_kernel, blocks, edge),
        in_specs=[smem] + [anywhere] * (blocks + 4),
        out_specs=[anywhere] * 4,
        out_shape=[out] * 4,
        input_output_aliases={1 + blocks + t: t for t in range(4)},
        scratch_shapes=[
            pltpu.VMEM((blocks, 4, BLOCK, last * HEAD), jnp.bfloat16),
            pltpu.SemaphoreType.DMA((blocks,)),
            pltpu.SemaphoreType.DMA((blocks, 4)),
        ],
        compiler_params=big,
        cost_estimate=huge,
    )(partner.astype(jnp.int32), *parts, *finals)
    patched = pl.pallas_call(
        functools.partial(patch_kernel, heads, blocks),
        in_specs=[smem, anywhere, vmem, vmem, anywhere, anywhere],
        out_specs=[anywhere] * 2,
        out_shape=[out] * 2,
        input_output_aliases={4: 0, 5: 1},
        scratch_shapes=[
            pltpu.VMEM((devices, 2 * blocks, width), jnp.bfloat16),
            pltpu.VMEM((2, blocks, BLOCK, width), jnp.bfloat16),
            pltpu.SemaphoreType.DMA(()),
            pltpu.SemaphoreType.DMA((2, blocks)),
            pltpu.SemaphoreType.DMA((2, blocks)),
        ],
        compiler_params=big,
    )(
        dilation_phase,
        got,
        new_cos.reshape(blocks, width),
        new_sin.reshape(blocks, width),
        finals[2],
        finals[3],
    )
    return finals[0], finals[1], patched[0], patched[1]


def solution(mesh):
    token = P(("groups", "ctx", "bal"), "head")
    return jax.shard_map(
        local,
        mesh=mesh,
        in_specs=(token, token, token, token, P("head"), P("head"), P("groups")),
        out_specs=(token, token, token, token),
        check_vma=False,
    )
```

time: 311 us -> 197 us (0.63)
  Pallas kernels: 175 us -> 72.4 us
  local copies, waits for them, and re-layouts: 16.7 us -> 7.24 us
  waiting for transfers between devices: 88.7 us -> 84.9 us
    pallas_call x2 -> x6, Pallas kernels: 127 us -> 44.8 us  [the longest x2 26.3 us: attend_relaid(): pl.pallas_call(functools.partial(attend_kernel, per_step, blocks, count,...]
    pallas_call x2 -> x1, Pallas kernels: 45.2 us -> 22.6 us  [local(): pl.pallas_call(functools.partial(attend_kernel, per_step, blocks, count,...]
    ppermute x6 -> x8, waiting for transfers between devices: 88.7 us -> 69.3 us  [swap(): return lax.ppermute(array, 'bal', [(i, i ^ k) for i in range(bal_size)])]
    all_to_all x1, waiting for transfers between devices: 0.01 us -> 15.6 us  [local(): lax.all_to_all(own_far, ('ctx', 'bal'), split_axis=0, concat_axis=0, tile...]
    unnamed x44 -> x46, local copies, waits for them, and re-layouts: 15.5 us -> 7.24 us
    ppermute x6 -> x8, starting transfers between devices: 4.01 us -> 7.29 us  [swap(): return lax.ppermute(array, 'bal', [(i, i ^ k) for i in range(bal_size)])]
  transfers between devices with their start and end apart: 8 -> 10, of which waited for: 4 -> 3; matrix products, arithmetic and copies ran while one was open for 3% -> 8% of each run, Pallas kernels for 46% -> 24%
where the time goes in v2:
time: 197 us; the launch traced here: 196 us
  waiting for transfers between devices  84.9 us (43%)
  Pallas kernels  72.4 us (37%)
  starting transfers between devices  16.5 us (8%)
  other arithmetic  13.9 us (7%)
  local copies, waits for them, and re-layouts  7.24 us (4%)
    ppermute x8, waiting for transfers between devices, swap(): return lax.ppermute(array, 'bal', [(i, i ^ k) for i in range(bal_size)])  69.3 us
    pallas_call x2, Pallas kernels, attend_relaid(): pl.pallas_call(functools.partial(attend_kernel, per_step, blocks, count,...  26.3 us
    pallas_call x1, Pallas kernels, local(): pl.pallas_call(functools.partial(attend_kernel, per_step, blocks, count,...  22.6 us
    all_to_all x1, waiting for transfers between devices, local(): lax.all_to_all(own_far, ('ctx', 'bal'), split_axis=0, concat_axis=0, tile...  15.6 us
    ppermute x8, starting transfers between devices, swap(): return lax.ppermute(array, 'bal', [(i, i ^ k) for i in range(bal_size)])  7.29 us
    unnamed x46, local copies, waits for them, and re-layouts  7.24 us
    pallas_call x2, Pallas kernels, send_inputs(): pl.pallas_call(functools.partial(pack_kernel, jobs), in_specs=[smem] + [a...  6.46 us
    pallas_call x1, Pallas kernels, local(): pl.pallas_call(functools.partial(patch_kernel, heads, blocks), in_specs=[...  6.38 us
  transfers between devices with their start and end apart: 10, of which 3 were waited for; matrix products, arithmetic and copies ran while one was open for 8% of the time, Pallas kernels for 24%

profile of v2, /device:TPU:0, one launch (start us, length us, event | category | flops | bytes accessed | tf_op | source)
XLA Modules:
  0.0 196.2 jit_solution(12367156363295158562)
XLA Ops:
  0.6 0.7 and_select_fusion.7
  2.8 2.9 %shard_map.102 = (bf16[4,128,512]{2,1,0:T(8,128)(2,1)}, bf16[4,128,512]{2,1,0:T(8,128)(2,1)}) custom-call(s32[8]{0:T(128)} %pad_add_fusion.1.info, s32[128]{0:T(128)} %after.1, bf16[512,2560]{1,0:T(8,128)(2,1)} %rest_4_.5, bf16[512,2560]{1,0:T(8,128)(2,1)} %rest_5_.5, bf16[512,2560]{1,0:T(8,128)(2,1)} %rest_6_.5, bf16[512,2560]{1,0:T(8,128)(2,1)} %rest_7_.5), custom_call_target="tpu_custom_call" | custom-call | tf_op jit(solution)/shard_map/pallas_call | solution.py:315
  5.7 2.4 %collective-permute-start.7 = (bf16[4,128,512]{2,1,0:T(8,128)(2,1)}, bf16[4,128,512]{2,1,0:T(8,128)(2,1)}, u32[]{:S(2)}, u32[]{:S(2)}) collective-permute-start(bf16[4,128,512]{2,1,0:T(8,128)(2,1)} %get-tuple-element.38), channel_id=1, source_target_pairs={{0,3},{1,2},{2,1},{3,0},{4,7},{5,6},{6,5},{7,4},{8,11},{9,10},{10,... | collective-permute-start | bytes 1572872 | tf_op jit(solution)/shard_map/ppermute | solution.py:292
  8.1 0.6 collective-permute-start.6
  11.6 5.0 %shard_map.103.after = bf16[32,8,2560]{2,1,0:T(8,128)(2,1)} custom-call(s32[20]{0:T(128)} %phase.9, bf16[512,2560]{1,0:T(8,128)(2,1)} %rest_5_.5, bf16[512,2560]{1,0:T(8,128)(2,1)} %rest_6_.5, f32[4,2560]{1,0:T(4,128)} %bitcast.44, f32[4,2560]{1,0:T(4,128)} %bitcast.45, bf16[4,128,512]{2,1,0:T(8,128)(2,1)} %get-tuple-element.30.after), custom_call_target="tpu_custom_call" | custom-call | tf_op jit(solution)/shard_map/pallas_call | solution.py:333
  16.6 5.8 %all-to-all-start = ((bf16[32,8,2560]{2,1,0:T(8,128)(2,1)}), bf16[32,8,2560]{2,1,0:T(8,128)(2,1)S(1)}, u32[]{:S(2)}, u32[]{:S(2)}) async-start(bf16[32,8,2560]{2,1,0:T(8,128)(2,1)} %shard_map.103.after), calls=%async_computation | async-start | bytes 2621440 | tf_op jit(solution)/shard_map/all_to_all | solution.py:354
  22.5 3.6 %shard_map.105 = (bf16[4,128,768]{2,1,0:T(8,128)(2,1)}, bf16[4,128,768]{2,1,0:T(8,128)(2,1)}, bf16[4,128,1280]{2,1,0:T(8,128)(2,1)}) custom-call(s32[8]{0:T(128)} %pad_add_fusion.1.info, bf16[32,8,2560]{2,1,0:T(8,128)(2,1)} %shard_map.103.after, bf16[512,2560]{1,0:T(8,128)(2,1)} %rest_4_.5, bf16[512,2560]{1,0:T(8,128)(2,1)} %rest_5_.5, ...), custom_call_target="tpu_custom_call" | custom-call | tf_op jit(solution)/shard_map/pallas_call | solution.py:315
  26.1 1.8 collective-permute-start.4
  29.5 2.1 %fusion.13 = (f32[512,64]{1,0:T(8,128)S(1)}, f32[512,64]{1,0:T(8,128)S(1)}, f32[512,64]{1,0:T(8,128)S(1)}, f32[512,64]{1,0:T(8,128)S(1)}, f32[512,64]{1,0:T(8,12...) fusion(f32[64]{0:T(128)S(1)} %copy-done.11, ...), kind=kLoop, calls=%fused_computation.33 | loop fusion | flops 589824 | bytes 1581568 | tf_op jit(solution)/shard_map/neg | solution.py:32
  31.5 0.9 pad_maximum_fusion.4.rest_0_
  32.4 0.8 pad_maximum_fusion.6.rest_2_
  33.2 0.9 pad_maximum_fusion.rest_0_
  34.1 0.8 pad_maximum_fusion.2.rest_2_
  34.9 0.8 pad_maximum_fusion.7.rest_3_
  35.8 0.8 pad_maximum_fusion.5.rest_1_
  36.6 0.8 pad_maximum_fusion.3.rest_3_
  37.4 0.8 pad_maximum_fusion.1.rest_1_
  38.3 0.8 fusion.10
  39.0 15.6 %all-to-all-done = bf16[32,8,2560]{2,1,0:T(8,128)(2,1)S(1)} async-done(((bf16[32,8,2560]{2,1,0:T(8,128)(2,1)}), bf16[32,8,2560]{2,1,0:T(8,128)(2,1)S(1)}, u32[]{:S(2)}, u32[]{:S(2)}) %all-to-all-start) | async-done | bytes 1310752 | tf_op jit(solution)/shard_map/all_to_all | solution.py:354
  54.7 1.1 copy-done
  55.7 22.6 %shard_map.104 = (bf16[4,128,1280]{2,1,0:T(8,128)(2,1)}, bf16[4,128,1280]{2,1,0:T(8,128)(2,1)}, bf16[4,128,1280]{2,1,0:T(8,128)(2,1)}, bf16[4,128,1280]{2,1,0:T(8,128)(2,1)}, bf16[256,2560]{1,0:T(8,128)(2,1)}) custom-call(s32[8]{0:T(128)} %pad_add_fusion.1.info, s32[20]{0:T(128)} %phase.9, s32[20]{0:T(128)} %seg.5, bf16[256,2560]{1,0:T(8,128)(2,1)} %bitcast.36, ...), custom_call_target="tpu_custom_call" | custom-call | flops 20000000000 | bytes 60000000 | tf_op jit(solution)/shard_map/pallas_call | solution.py:386
  78.4 1.1 copy-done.1
  79.4 11.1 %shard_map.106 = (bf16[4,128,2560]{2,1,0:T(8,128)(2,1)}, bf16[4,128,2560]{2,1,0:T(8,128)(2,1)}, bf16[4,128,2560]{2,1,0:T(8,128)(2,1)}, bf16[4,128,2560]{2,1,0:T(8,128)(2,1)}, bf16[256,2560]{1,0:T(8,128)(2,1)}) custom-call(s32[12]{0:T(128)} %pad_add_fusion.2.info, s32[20]{0:T(128)} %phase.9, s32[20]{0:T(128)} %seg.5, ...), custom_call_target="tpu_custom_call", output_to_operand_aliasing={{4}: (17, {})} | custom-call | flops 2000000000 | bytes 5000000 | tf_op jit(solution)/shard_map/pallas_call | solution.py:420
  90.6 0.9 copy-done.4
  91.4 15.2 %shard_map.107 = (bf16[4,128,2560]{2,1,0:T(8,128)(2,1)}, bf16[4,128,2560]{2,1,0:T(8,128)(2,1)}, bf16[4,128,2560]{2,1,0:T(8,128)(2,1)}, bf16[4,128,2560]{2,1,0:T(8,128)(2,1)}, bf16[256,2560]{1,0:T(8,128)(2,1)}) custom-call(s32[12]{0:T(128)} %pad_add_fusion.2.info, ...), custom_call_target="tpu_custom_call", output_to_operand_aliasing={{0}: (17, {}), {1}: (18, {}), {2}: (19, {}), {3}: (20, {}),... | custom-call | flops 2000000000 | bytes 5000000 | tf_op jit(solution)/shard_map/pallas_call | solution.py:420
  106.7 3.5 %all-to-all-start.1 = ((bf16[32,8,2560]{2,1,0:T(8,128)(2,1)}), bf16[32,8,2560]{2,1,0:T(8,128)(2,1)S(1)}, u32[]{:S(2)}, u32[]{:S(2)}) async-start(bf16[32,8,2560]{2,1,0:T(8,128)(2,1)} %bitcast.39), calls=%async_computation.1 | async-start | bytes 2621440 | tf_op jit(solution)/shard_map/all_to_all | solution.py:459
  110.5 1.7 collective-permute-start.1
  113.6 42.1 %collective-permute-done.1.rest_2_ = bf16[4,128,1280]{2,1,0:T(8,128)(2,1)} collective-permute-done((bf16[4,128,1280]{2,1,0:T(8,128)(2,1)}, bf16[4,128,1280]{2,1,0:T(8,128)(2,1)}, u32[]{:S(2)}, u32[]{:S(2)}) %collective-permute-start.1) | collective-permute-done | bytes 1310752 | tf_op jit(solution)/shard_map/ppermute | solution.py:292
  155.7 27.1 %collective-permute-done.2.rest_3_ = bf16[4,128,1280]{2,1,0:T(8,128)(2,1)} collective-permute-done((bf16[4,128,1280]{2,1,0:T(8,128)(2,1)}, bf16[4,128,1280]{2,1,0:T(8,128)(2,1)}, u32[]{:S(2)}, u32[]{:S(2)}) %collective-permute-start.2) | collective-permute-done | bytes 1310752 | tf_op jit(solution)/shard_map/ppermute | solution.py:292
  182.8 5.7 %shard_map.108 = (bf16[512,2560]{1,0:T(8,128)(2,1)}, bf16[512,2560]{1,0:T(8,128)(2,1)}, bf16[512,2560]{1,0:T(8,128)(2,1)}, bf16[512,2560]{1,0:T(8,128)(2,1)}) custom-call(s32[4]{0:T(128)} %copy-done.8, bf16[4,128,1280]{2,1,0:T(8,128)(2,1)} %get-tuple-element.31.rest_0_, ...), custom_call_target="tpu_custom_call", output_to_operand_aliasing={{0}: (5, {}), {1}: (6, {}), {2}: (7, {}), {3}: (8, {})} | custom-call | flops 1000 | bytes 400000000 | tf_op jit(solution)/shard_map/pallas_call | solution.py:470
  188.5 1.1 copy-done.2
  189.6 6.4 %shard_map.109 = (bf16[512,2560]{1,0:T(8,128)(2,1)}, bf16[512,2560]{1,0:T(8,128)(2,1)}) custom-call(s32[20]{0:T(128)} %phase.9, bf16[32,8,2560]{2,1,0:T(8,128)(2,1)} %copy-done.2, f32[4,2560]{1,0:T(4,128)} %bitcast.43, f32[4,2560]{1,0:T(4,128)} %bitcast.42, bf16[512,2560]{1,0:T(8,128)(2,1)} %get-tuple-element.52.dk_in, ...), custom_call_target="tpu_custom_call", output_to_operand_aliasing={{0}: (4, {}), {1}: (5, {})} | custom-call | tf_op jit(solution)/shard_map/pallas_call | solution.py:484
  (78 shorter events, 7.5 us)
Async XLA Ops:
  1.4 0.5 copy-start.8
  1.6 0.5 copy-start.16
  2.8 6.0 %copy-start.14 = (s32[128]{0:T(128)S(1)}, s32[128]{0:T(128)}, u32[]{:S(2)}) copy-start(s32[128]{0:T(128)} %after.1) | copy-start | bytes 1540
  2.8 6.8 %copy-start.5 = (s32[20]{0:T(128)S(1)}, s32[20]{0:T(128)}, u32[]{:S(2)}) copy-start(s32[20]{0:T(128)} %phase.9) | copy-start | bytes 244
  5.7 72.7 %collective-permute-start.7 = (bf16[4,128,512]{2,1,0:T(8,128)(2,1)}, bf16[4,128,512]{2,1,0:T(8,128)(2,1)}, u32[]{:S(2)}, u32[]{:S(2)}) collective-permute-start(bf16[4,128,512]{2,1,0:T(8,128)(2,1)} %get-tuple-element.38), channel_id=1, source_target_pairs={{0,3},{1,2},{2,1},{3,0},{4,7},{5,6},{6,5},{7,4},{8,11},{9,10},{10,... | collective-permute-start | bytes 1572872 | tf_op jit(solution)/shard_map/ppermute | solution.py:292
  8.1 70.2 %collective-permute-start.6 = (bf16[4,128,512]{2,1,0:T(8,128)(2,1)}, bf16[4,128,512]{2,1,0:T(8,128)(2,1)}, u32[]{:S(2)}, u32[]{:S(2)}) collective-permute-start(bf16[4,128,512]{2,1,0:T(8,128)(2,1)} %get-tuple-element.30.after), channel_id=1, source_target_pairs={{0,2},{1,3},{2,0},{3,1},{4,6},{5,7},{6,4},{7,5},{8,10},{9,11},{10,... | collective-permute-start | bytes 1572872 | tf_op jit(solution)/shard_map/ppermute | solution.py:292
  8.7 1.0 copy-start.6
  8.8 2.8 %copy-start.10 = (f32[64]{0:T(128)}, f32[64]{0:T(128)S(1)}, u32[]{:S(2)}) copy-start(f32[64]{0:T(128)S(1)} %get-tuple-element.95) | copy-start | bytes 772
  8.8 2.8 %copy-start.12 = (f32[64]{0:T(128)}, f32[64]{0:T(128)S(1)}, u32[]{:S(2)}) copy-start(f32[64]{0:T(128)S(1)} %get-tuple-element.96) | copy-start | bytes 772
  9.0 0.6 copy-start.18
  16.6 38.0 %all-to-all-start = ((bf16[32,8,2560]{2,1,0:T(8,128)(2,1)}), bf16[32,8,2560]{2,1,0:T(8,128)(2,1)S(1)}, u32[]{:S(2)}, u32[]{:S(2)}) async-start(bf16[32,8,2560]{2,1,0:T(8,128)(2,1)} %shard_map.103.after), calls=%async_computation | async-start | bytes 2621440 | tf_op jit(solution)/shard_map/all_to_all | solution.py:354
  22.4 5.9 %copy-start.15 = (s32[128]{0:T(128)S(1)}, s32[128]{0:T(128)}, u32[]{:S(2)}) copy-start(s32[128]{0:T(128)} %after.1) | copy-start | bytes 1540
  22.4 5.9 %copy-start.19 = (s32[4]{0:T(128)S(1)}, s32[4]{0:T(128)}, u32[]{:S(2)}) copy-start(s32[4]{0:T(128)} %copy-done.18) | copy-start | bytes 52
  22.4 5.9 %copy-start.20 = (s32[4]{0:T(128)S(1)}, s32[4]{0:T(128)}, u32[]{:S(2)}) copy-start(s32[4]{0:T(128)} %get-tuple-element.90) | copy-start | bytes 52
  22.5 6.1 %copy-start.9 = (s32[4]{0:T(128)S(1)}, s32[4]{0:T(128)}, u32[]{:S(2)}) copy-start(s32[4]{0:T(128)} %copy-done.8) | copy-start | bytes 52
  22.5 6.1 %copy-start.17 = (s32[4]{0:T(128)S(1)}, s32[4]{0:T(128)}, u32[]{:S(2)}) copy-start(s32[4]{0:T(128)} %copy-done.16) | copy-start | bytes 52
  22.5 6.8 %copy-start.7 = (s32[4]{0:T(128)S(1)}, s32[4]{0:T(128)}, u32[]{:S(2)}) copy-start(s32[4]{0:T(128)} %copy-done.6) | copy-start | bytes 52
  22.5 7.0 %copy-start.11 = (f32[64]{0:T(128)S(1)}, f32[64]{0:T(128)}, u32[]{:S(2)}) copy-start(f32[64]{0:T(128)} %copy-done.10) | copy-start | bytes 772
  22.5 7.0 %copy-start.13 = (f32[64]{0:T(128)S(1)}, f32[64]{0:T(128)}, u32[]{:S(2)}) copy-start(f32[64]{0:T(128)} %copy-done.12) | copy-start | bytes 772
  26.1 64.5 %collective-permute-start.4 = (bf16[4,128,768]{2,1,0:T(8,128)(2,1)}, bf16[4,128,768]{2,1,0:T(8,128)(2,1)S(1)}, u32[]{:S(2)}, u32[]{:S(2)}) collective-permute-start(bf16[4,128,768]{2,1,0:T(8,128)(2,1)} %get-tuple-element.36), channel_id=1, source_target_pairs={{0,2},{1,3},{2,0},{3,1},{4,6},{5,7},{6,4},{7,5},{8,10},{9,11},{10,... | collective-permute-start | bytes 2359304 | tf_op jit(solution)/shard_map/ppermute | solution.py:292
  27.9 62.6 %collective-permute-start.5 = (bf16[4,128,768]{2,1,0:T(8,128)(2,1)}, bf16[4,128,768]{2,1,0:T(8,128)(2,1)}, u32[]{:S(2)}, u32[]{:S(2)}) collective-permute-start(bf16[4,128,768]{2,1,0:T(8,128)(2,1)} %get-tuple-element.37), channel_id=1, source_target_pairs={{0,3},{1,2},{2,1},{3,0},{4,7},{5,6},{6,5},{7,4},{8,11},{9,10},{10,... | collective-permute-start | bytes 2359304 | tf_op jit(solution)/shard_map/ppermute | solution.py:292
  27.9 50.4 %collective-permute-start.3 = (bf16[4,128,1280]{2,1,0:T(8,128)(2,1)}, bf16[4,128,1280]{2,1,0:T(8,128)(2,1)S(1)}, u32[]{:S(2)}, u32[]{:S(2)}) collective-permute-start(bf16[4,128,1280]{2,1,0:T(8,128)(2,1)} %get-tuple-element.35), channel_id=1, source_target_pairs={{0,1},{1,0},{2,3},{3,2},{4,5},{5,4},{6,7},{7,6},{8,9},{9,8},{10,11... | collective-permute-start | bytes 3932168 | tf_op jit(solution)/shard_map/ppermute | solution.py:292
  54.7 1.1 copy-start
  78.4 1.1 copy-start.1
  90.5 0.9 copy-start.4
  106.7 81.9 %all-to-all-start.1 = ((bf16[32,8,2560]{2,1,0:T(8,128)(2,1)}), bf16[32,8,2560]{2,1,0:T(8,128)(2,1)S(1)}, u32[]{:S(2)}, u32[]{:S(2)}) async-start(bf16[32,8,2560]{2,1,0:T(8,128)(2,1)} %bitcast.39), calls=%async_computation.1 | async-start | bytes 2621440 | tf_op jit(solution)/shard_map/all_to_all | solution.py:459
  110.1 3.4 %collective-permute-start = (bf16[4,128,1280]{2,1,0:T(8,128)(2,1)}, bf16[4,128,1280]{2,1,0:T(8,128)(2,1)S(1)}, u32[]{:S(2)}, u32[]{:S(2)}) collective-permute-start(bf16[4,128,1280]{2,1,0:T(8,128)(2,1)} %get-tuple-element.32), channel_id=1, source_target_pairs={{0,1},{1,0},{2,3},{3,2},{4,5},{5,4},{6,7},{7,6},{8,9},{9,8},{10,11... | collective-permute-start | bytes 3932168 | tf_op jit(solution)/shard_map/ppermute | solution.py:292
  110.5 45.3 %collective-permute-start.1 = (bf16[4,128,1280]{2,1,0:T(8,128)(2,1)}, bf16[4,128,1280]{2,1,0:T(8,128)(2,1)}, u32[]{:S(2)}, u32[]{:S(2)}) collective-permute-start(bf16[4,128,1280]{2,1,0:T(8,128)(2,1)} %get-tuple-element.33), channel_id=1, source_target_pairs={{0,2},{1,3},{2,0},{3,1},{4,6},{5,7},{6,4},{7,5},{8,10},{9,11},{10,... | collective-permute-start | bytes 3932168 | tf_op jit(solution)/shard_map/ppermute | solution.py:292
  112.1 70.7 %collective-permute-start.2 = (bf16[4,128,1280]{2,1,0:T(8,128)(2,1)}, bf16[4,128,1280]{2,1,0:T(8,128)(2,1)}, u32[]{:S(2)}, u32[]{:S(2)}) collective-permute-start(bf16[4,128,1280]{2,1,0:T(8,128)(2,1)} %get-tuple-element.34), channel_id=1, source_target_pairs={{0,3},{1,2},{2,1},{3,0},{4,7},{5,6},{6,5},{7,4},{8,11},{9,10},{10,... | collective-permute-start | bytes 3932168 | tf_op jit(solution)/shard_map/ppermute | solution.py:292
  113.6 69.3 %copy-start.3 = (bf16[4,128,1280]{2,1,0:T(8,128)(2,1)}, bf16[4,128,1280]{2,1,0:T(8,128)(2,1)S(1)}, u32[]{:S(2)}) copy-start(bf16[4,128,1280]{2,1,0:T(8,128)(2,1)S(1)} %collective-permute-done.rest_1_) | copy-start | bytes 3932164
  188.5 1.1 copy-start.2
